TPU v7x, 32 devices: a whole 2x2x4 slice. The times are simulated.
32 devices in a mesh: section: 2 (over y), dp: 16 (over z, x, core).
Axes of the slice: x: 2, y: 2, z: 4, core: 2. Of those that a mesh axis runs over, the one named last changes fastest.
Arguments:
- tokens: bfloat16 [64, 64, 768], P('dp'), may hold values from -6 to 6
- images: bfloat16 [64, 256, 768], P('dp', 'section'), may hold values from -6 to 6
- lengths: int32 [64], P('dp'), may hold values from 5 to 64, as said below
- cotangent: bfloat16 [2, 64, 64, 768], P('section', 'dp'), may hold values from -6 to 6
- attend_gain: float32 [2, 768], P('section'), may hold values from 0.5 to 1.5
- attend_shift: float32 [2, 768], P('section'), may hold values from -2 to 2
- projections: bfloat16 [2, 768, 2304], P('section'), may hold values from -0.21875 to 0.21875
- query_bias: float32 [2, 768], P('section'), may hold values from -3 to 3
- value_bias: float32 [2, 768], P('section'), may hold values from -2 to 2
- output_weight: bfloat16 [2, 768, 768], P('section'), may hold values from -0.625 to 0.625
- output_bias: float32 [2, 768], P('section'), may hold values from -2 to 2
- feed_gain: float32 [2, 768], P('section'), may hold values from 0.5 to 1.5
- feed_shift: float32 [2, 768], P('section'), may hold values from -2 to 2
- expand_weight: bfloat16 [2, 768, 3072], P('section'), may hold values from -0.21875 to 0.21875
- expand_bias: float32 [2, 3072], P('section'), may hold values from -3 to 3
- reduce_weight: bfloat16 [2, 3072, 768], P('section'), may hold values from -0.21875 to 0.21875
- reduce_bias: float32 [2, 768], P('section'), may hold values from -2 to 2
- cross_gain: float32 [768], replicated, may hold values from 0.5 to 1.5
- cross_shift: float32 [768], replicated, may hold values from -2 to 2
- cross_query: bfloat16 [768, 768], replicated, may hold values from -0.21875 to 0.21875
- cross_query_bias: float32 [768], replicated, may hold values from -3 to 3
- cross_key: bfloat16 [768, 768], replicated, may hold values from -0.21875 to 0.21875
- cross_value: bfloat16 [768, 768], replicated, may hold values from -0.21875 to 0.21875
- cross_value_bias: float32 [768], replicated, may hold values from -2 to 2
- cross_out: bfloat16 [768, 768], replicated, may hold values from -1.25 to 1.25
- cross_out_bias: float32 [768], replicated, may hold values from -2 to 2
Outputs:
- layer_outputs: bfloat16 [2, 64, 64, 768], P('section', 'dp')
- input_gradient: float32 [2, 64, 64, 768], P('section', 'dp')
- image_gradient: float32 [64, 256, 768], P('dp', 'section')
- attend_gain_gradient: float32 [2, 768], P('section', 'dp')
- attend_shift_gradient: float32 [2, 768], P('section', 'dp')
- projections_gradient: float32 [2, 768, 2304], P('section', 'dp')
- query_bias_gradient: float32 [2, 768], P('section', 'dp')
- value_bias_gradient: float32 [2, 768], P('section', 'dp')
- output_weight_gradient: float32 [2, 768, 768], P('section', 'dp')
- output_bias_gradient: float32 [2, 768], P('section', 'dp')
- feed_gain_gradient: float32 [2, 768], P('section', 'dp')
- feed_shift_gradient: float32 [2, 768], P('section', 'dp')
- expand_weight_gradient: float32 [2, 768, 3072], P('section', 'dp')
- expand_bias_gradient: float32 [2, 3072], P('section', 'dp')
- reduce_weight_gradient: float32 [2, 3072, 768], P('section', 'dp')
- reduce_bias_gradient: float32 [2, 768], P('section', 'dp')
- cross_gain_gradient: float32 [768], P('dp')
- cross_shift_gradient: float32 [768], P('dp')
- cross_query_gradient: float32 [768, 768], P('dp')
- cross_query_bias_gradient: float32 [768], P('dp')
- cross_key_gradient: float32 [768, 768], P('dp')
- cross_value_gradient: float32 [768, 768], P('dp')
- cross_value_bias_gradient: float32 [768], P('dp')
- cross_out_gradient: float32 [768, 768], P('dp')
- cross_out_bias_gradient: float32 [768], P('dp')
Inputs may be any that keep to these rules, and one draw needn't show every extreme that they name: `lengths`: some caption uses all 64 slots and some caption uses 5.
All inputs are finite; a program needn't handle non-finite values.
Results may differ from a plain program's by a relative error of at most 0.023.
Values may be sent and summed in bfloat16 or wider, within the bound.
A program may use at most 320 MiB of HBM per device.

v0:
```python
import jax
import jax.numpy as jnp
from jax import lax
from jax.sharding import PartitionSpec as P

HEADS = 12
HEAD_DIM = 64
MB_CAPS = 1
MICRO = 4


EPS = 1e-05
NEG = -1000000000.0


def shifted(block, axis, distance):
    devices = range(lax.axis_size(axis))
    route = [(i - distance, i) for i in devices if i - distance in devices]
    return lax.ppermute(block, axis, route)


def for_sending(array):
    return jax.tree.map(lambda a: a.astype(jnp.bfloat16) if a.dtype == jnp.float32 else a, array)


def layer_norm(rows, gain, shift):
    mean = jnp.mean(rows, -1, keepdims=True)
    centred = rows - mean
    inverse = lax.rsqrt(jnp.mean(centred * centred, -1, keepdims=True) + EPS)
    normed = centred * inverse
    return (normed * gain + shift, normed, inverse)


def norm_back(grad, normed, inverse, gain):
    scaled = grad * gain
    inner = (
        scaled
        - jnp.mean(scaled, -1, keepdims=True)
        - normed * jnp.mean(scaled * normed, -1, keepdims=True)
    )
    return (inverse * inner, jnp.sum(grad * normed, axis=(0, 1)), jnp.sum(grad, axis=(0, 1)))


def product(rows, weight):
    return jnp.einsum("bsi,ij->bsj", rows, weight, preferred_element_type=jnp.float32)


def back_product(grad, weight):
    return jnp.einsum("bsj,ij->bsi", grad, weight, preferred_element_type=jnp.float32)


def weight_product(rows, grad):
    return jnp.einsum("bsi,bsj->ij", rows, grad, preferred_element_type=jnp.float32)


def column_sum(grad):
    return jnp.sum(grad.astype(jnp.float32), axis=(0, 1))


def split_heads(rows):
    return rows.reshape(rows.shape[0], rows.shape[1], HEADS, HEAD_DIM)


def scores_of(query, keys, mask):
    scores = jnp.einsum(
        "bqhd,bkhd->bhqk", split_heads(query), split_heads(keys), preferred_element_type=jnp.float32
    ) * HEAD_DIM ** (-0.5)
    if mask is None:
        return scores
    return jnp.where(mask[:, None], scores, NEG)


def attend(query, keys, values, mask):
    scores = scores_of(query, keys, mask)
    top = jnp.max(scores, -1, keepdims=True)
    expo = jnp.exp(scores - top)
    total = jnp.sum(expo, -1, keepdims=True)
    probs = (expo / total).astype(jnp.bfloat16)
    mixed = jnp.einsum(
        "bhqk,bkhd->bqhd", probs, split_heads(values), preferred_element_type=jnp.float32
    )
    return (mixed.reshape(query.shape).astype(jnp.bfloat16), top + jnp.log(total))


def attend_back(grad, query, keys, values, logsum, mask):
    scale = HEAD_DIM ** (-0.5)
    probs = jnp.exp(scores_of(query, keys, mask) - logsum)
    grad_heads = split_heads(grad)
    dprobs = jnp.einsum(
        "bqhd,bkhd->bhqk", grad_heads, split_heads(values), preferred_element_type=jnp.float32
    )
    rowdot = jnp.sum(probs * dprobs, -1, keepdims=True)
    dscores = (probs * (dprobs - rowdot)).astype(jnp.bfloat16)
    dquery = (
        jnp.einsum(
            "bhqk,bkhd->bqhd", dscores, split_heads(keys), preferred_element_type=jnp.float32
        )
        * scale
    )
    dkeys = (
        jnp.einsum(
            "bhqk,bqhd->bkhd", dscores, split_heads(query), preferred_element_type=jnp.float32
        )
        * scale
    )
    dvalues = jnp.einsum(
        "bhqk,bqhd->bkhd",
        probs.astype(jnp.bfloat16),
        grad_heads,
        preferred_element_type=jnp.float32,
    )
    return (
        dquery.reshape(query.shape).astype(jnp.bfloat16),
        dkeys.reshape(keys.shape).astype(jnp.bfloat16),
        dvalues.reshape(values.shape).astype(jnp.bfloat16),
    )


def self_forward(hidden, layer, mask):
    normal, normed, inverse = layer_norm(hidden, layer[0], layer[1])
    entry = normal.astype(jnp.bfloat16)
    packed = product(entry, layer[2])
    width = hidden.shape[-1]
    query = (packed[..., :width] + layer[3]).astype(jnp.bfloat16)
    keys = packed[..., width : 2 * width].astype(jnp.bfloat16)
    values = (packed[..., 2 * width :] + layer[4]).astype(jnp.bfloat16)
    mixed, logsum = attend(query, keys, values, mask)
    after = hidden + (product(mixed, layer[5]) + layer[6])
    return (after, (normed, inverse, entry, query, keys, values, mixed, logsum))


def self_back(grad, saved, layer, mask):
    normed, inverse, entry, query, keys, values, mixed, logsum = saved
    branch = grad.astype(jnp.bfloat16)
    out_weight_grad = weight_product(mixed, branch)
    out_bias_grad = column_sum(branch)
    dmixed = back_product(branch, layer[5]).astype(jnp.bfloat16)
    dquery, dkeys, dvalues = attend_back(dmixed, query, keys, values, logsum, mask)
    dpacked = jnp.concatenate([dquery, dkeys, dvalues], -1)
    packed_grad = weight_product(entry, dpacked)
    dentry = back_product(dpacked, layer[2])
    dhidden, gain_grad, shift_grad = norm_back(dentry, normed, inverse, layer[0])
    return (
        grad + dhidden,
        (
            gain_grad,
            shift_grad,
            packed_grad,
            column_sum(dquery),
            column_sum(dvalues),
            out_weight_grad,
            out_bias_grad,
        ),
    )


def gelu_slope(expanded):
    normal_cdf = 0.5 * (1.0 + jax.scipy.special.erf(expanded * 0.7071067811865476))
    return normal_cdf + expanded * jnp.exp(-0.5 * expanded * expanded) * 0.3989422804014327


def feed_forward(hidden, layer):
    normal, normed, inverse = layer_norm(hidden, layer[7], layer[8])
    entry = normal.astype(jnp.bfloat16)
    expanded = product(entry, layer[9]) + layer[10]
    active = jax.nn.gelu(expanded, approximate=False).astype(jnp.bfloat16)
    after = hidden + (product(active, layer[11]) + layer[12])
    return (after, (normed, inverse, entry, expanded, active))


def feed_back(grad, saved, layer):
    normed, inverse, entry, expanded, active = saved
    branch = grad.astype(jnp.bfloat16)
    reduce_grad = weight_product(active, branch)
    reduce_bias_grad = column_sum(branch)
    dactive = back_product(branch, layer[11])
    dexpanded = (dactive * gelu_slope(expanded)).astype(jnp.bfloat16)
    expand_grad = weight_product(entry, dexpanded)
    expand_bias_grad = column_sum(dexpanded)
    dentry = back_product(dexpanded, layer[9])
    dhidden, gain_grad, shift_grad = norm_back(dentry, normed, inverse, layer[7])
    return (
        grad + dhidden,
        (gain_grad, shift_grad, expand_grad, expand_bias_grad, reduce_grad, reduce_bias_grad),
    )


def cross_forward(hidden, pairs, cross):
    normal, normed, inverse = layer_norm(hidden, cross[0], cross[1])
    entry = normal.astype(jnp.bfloat16)
    query = (product(entry, cross[2]) + cross[3]).astype(jnp.bfloat16)
    width = hidden.shape[-1]
    mixed, logsum = attend(query, pairs[..., :width], pairs[..., width:], None)
    after = hidden + (product(mixed, cross[7]) + cross[8])
    return (after, (normed, inverse, entry, query, mixed, logsum))


def cross_back(grad, saved, pairs, cross):
    normed, inverse, entry, query, mixed, logsum = saved
    width = grad.shape[-1]
    branch = grad.astype(jnp.bfloat16)
    out_grad = weight_product(mixed, branch)
    out_bias_grad = column_sum(branch)
    dmixed = back_product(branch, cross[7]).astype(jnp.bfloat16)
    dquery, dkeys, dvalues = attend_back(
        dmixed, query, pairs[..., :width], pairs[..., width:], logsum, None
    )
    query_grad = weight_product(entry, dquery)
    dentry = back_product(dquery, cross[2])
    dhidden, gain_grad, shift_grad = norm_back(dentry, normed, inverse, cross[0])
    parts = (gain_grad, shift_grad, query_grad, column_sum(dquery), out_grad, out_bias_grad)
    return (grad + dhidden, parts, jnp.concatenate([dkeys, dvalues], -1))


def body(
    tokens,
    images,
    lengths,
    cotangent,
    attend_gain,
    attend_shift,
    projections,
    query_bias,
    value_bias,
    output_weight,
    output_bias,
    feed_gain,
    feed_shift,
    expand_weight,
    expand_bias,
    reduce_weight,
    reduce_bias,
    cross_gain,
    cross_shift,
    cross_query,
    cross_query_bias,
    cross_key,
    cross_value,
    cross_value_bias,
    cross_out,
    cross_out_bias,
):
    layer = tuple(
        (
            weight[0]
            for weight in (
                attend_gain,
                attend_shift,
                projections,
                query_bias,
                value_bias,
                output_weight,
                output_bias,
                feed_gain,
                feed_shift,
                expand_weight,
                expand_bias,
                reduce_weight,
                reduce_bias,
            )
        )
    )
    cross = (
        cross_gain,
        cross_shift,
        cross_query,
        cross_query_bias,
        cross_key,
        cross_value,
        cross_value_bias,
        cross_out,
        cross_out_bias,
    )
    pair_weight = jnp.concatenate([cross_key, cross_value], 1)
    pair_bias = jnp.concatenate([jnp.zeros_like(cross_value_bias), cross_value_bias], 0)
    section_index = lax.axis_index("section")
    is_two = section_index == 1
    block = MB_CAPS
    half = images.shape[1]
    slots = tokens.shape[1]
    width = tokens.shape[2]
    positions = jnp.arange(slots, dtype=jnp.int32)
    causal = positions[None, :] <= positions[:, None]
    zero_cross = tuple((jnp.zeros(weight.shape, jnp.float32) for weight in cross))

    def image_project(image_rows):
        return (product(image_rows, pair_weight) + pair_bias).astype(jnp.bfloat16)

    def image_back(image_rows, dpairs):
        dimages = back_product(dpairs, pair_weight)
        pair_grad = weight_product(image_rows, dpairs)
        return (
            dimages,
            (pair_grad[:, :width], pair_grad[:, width:], column_sum(dpairs[..., width:])),
        )

    def cross_yes(hidden, image_data):
        pairs = image_project(image_data)
        after, saved = cross_forward(hidden, pairs, cross)
        return (after, saved, pairs)

    def cross_no(hidden, image_data):
        saved = (
            jnp.zeros((block, slots, width), jnp.float32),
            jnp.zeros((block, slots, 1), jnp.float32),
            jnp.zeros((block, slots, width), jnp.bfloat16),
            jnp.zeros((block, slots, width), jnp.bfloat16),
            jnp.zeros((block, slots, width), jnp.bfloat16),
            jnp.zeros((block, HEADS, slots, 1), jnp.float32),
        )
        return (hidden, saved, jnp.zeros((block, 2 * half, 2 * width), jnp.bfloat16))

    def back_yes(grad, saved, pairs, image_data):
        dgrad, parts, dpairs = cross_back(grad, saved, pairs, cross)
        dimages, image_terms = image_back(image_data, dpairs)
        return (dgrad, parts[:4] + image_terms + parts[4:], dimages)

    def back_no(grad, saved, pairs, image_data):
        return (grad, zero_cross, jnp.zeros((block, 2 * half, width), jnp.float32))

    received = jnp.zeros((block, slots, width), jnp.bfloat16)
    arriving = jnp.zeros((block, half, width), jnp.bfloat16)
    finished = jnp.zeros(tokens.shape, jnp.bfloat16)
    kept = []
    for tick in range(MICRO + 1):
        index = jnp.clip(tick - section_index, 0, MICRO - 1)
        start = index * block
        live = positions[None, :] < lax.dynamic_slice_in_dim(lengths, start, block, 0)[:, None]
        mask = live[:, None, :] & causal[None]
        own_tokens = lax.dynamic_slice_in_dim(tokens, start, block, 0)
        own_images = lax.dynamic_slice_in_dim(images, start, block, 0)
        hidden = jnp.where(is_two, received, own_tokens).astype(jnp.float32)
        after_self, self_saved = self_forward(hidden, layer, mask)
        image_data = jnp.concatenate([arriving, own_images], 1)
        after_cross, cross_saved, pairs = lax.cond(
            is_two, cross_yes, cross_no, after_self, image_data
        )
        final, feed_saved = feed_forward(after_cross, layer)
        result = final.astype(jnp.bfloat16)
        finished = lax.dynamic_update_slice_in_dim(finished, result, start, 0)
        kept.append((mask, live, self_saved, cross_saved, feed_saved, pairs, image_data))
        if tick < MICRO:
            received = shifted(result, "section", 1)
            arriving = shifted(own_images, "section", 1)
    layer_sums = tuple((jnp.zeros(weight.shape, jnp.float32) for weight in layer))
    cross_sums = zero_cross
    input_grads = jnp.zeros(tokens.shape, jnp.float32)
    image_grads = jnp.zeros(images.shape, jnp.float32)
    returning = jnp.zeros((block, slots, width), jnp.bfloat16)
    coming = jnp.zeros((block, half, width), jnp.float32)
    for turn in range(MICRO + 1):
        tick = MICRO - turn
        offset = tick - section_index
        index = jnp.clip(offset, 0, MICRO - 1)
        start = index * block
        valid = ((offset >= 0) & (offset < MICRO)).astype(jnp.float32)
        mask, live, self_saved, cross_saved, feed_saved, pairs, image_data = kept[tick]
        own_images = lax.dynamic_slice_in_dim(images, start, block, 0)
        seed_grad = lax.dynamic_slice_in_dim(cotangent[0], start, block, 0).astype(
            jnp.float32
        ) * live[..., None].astype(jnp.float32)
        grad = seed_grad + returning.astype(jnp.float32)
        grad, feed_grads = feed_back(grad, feed_saved, layer)
        grad, cross_grads, image_part = lax.cond(
            is_two, back_yes, back_no, grad, cross_saved, pairs, image_data
        )
        grad, self_grads = self_back(grad, self_saved, layer, mask)
        layer_sums = tuple(
            (total + valid * part for total, part in zip(layer_sums, self_grads + feed_grads))
        )
        cross_sums = tuple((total + valid * part for total, part in zip(cross_sums, cross_grads)))
        sent = grad.astype(jnp.bfloat16)
        stored = jnp.where(is_two, sent.astype(jnp.float32), grad)
        input_grads = jnp.where(
            valid > 0, lax.dynamic_update_slice_in_dim(input_grads, stored, start, 0), input_grads
        )
        own_dimages = jnp.where(is_two, image_part[:, half:], coming)
        image_grads = jnp.where(
            valid > 0,
            lax.dynamic_update_slice_in_dim(image_grads, own_dimages, start, 0),
            image_grads,
        )
        if turn < MICRO:
            returning = shifted(sent, "section", -1)
            coming = shifted(image_part[:, :half].astype(jnp.bfloat16), "section", -1).astype(
                jnp.float32
            )
    shared = lax.psum_scatter(
        tuple((total[None] for total in layer_sums)), "dp", scatter_dimension=1, tiled=True
    )
    scattered = lax.psum_scatter(cross_sums, "dp", scatter_dimension=0, tiled=True)
    crossed = jax.tree.map(
        lambda part: part.astype(jnp.float32), lax.psum(for_sending(tuple(scattered)), "section")
    )
    return (finished[None], input_grads[None], image_grads) + tuple(shared) + tuple(crossed)


def solution(mesh):
    placed = (
        P("dp", None, None),
        P("dp", "section", None),
        P("dp"),
        P("section", "dp", None, None),
        P("section", None),
        P("section", None),
        P("section", None, None),
        P("section", None),
        P("section", None),
        P("section", None, None),
        P("section", None),
        P("section", None),
        P("section", None),
        P("section", None, None),
        P("section", None),
        P("section", None, None),
        P("section", None),
        P(),
        P(),
        P(),
        P(),
        P(),
        P(),
        P(),
        P(),
        P(),
    )
    return jax.shard_map(
        body,
        mesh=mesh,
        in_specs=placed,
        out_specs=(
            P("section", "dp", None, None),
            P("section", "dp", None, None),
            P("dp", "section", None),
            P("section", "dp"),
            P("section", "dp"),
            P("section", "dp", None),
            P("section", "dp"),
            P("section", "dp"),
            P("section", "dp", None),
            P("section", "dp"),
            P("section", "dp"),
            P("section", "dp"),
            P("section", "dp", None),
            P("section", "dp"),
            P("section", "dp", None),
            P("section", "dp"),
            P("dp"),
            P("dp"),
            P("dp", None),
            P("dp"),
            P("dp", None),
            P("dp", None),
            P("dp"),
            P("dp", None),
            P("dp"),
        ),
        check_vma=False,
    )
```

profile of v0, /device:TPU:0, one launch (start us, length us, event | category | flops | bytes accessed | tf_op | source)
XLA Modules:
  0.0 1938.4 jit_solution(13967454048151218085)
XLA Ops:
  62.9 23.2 %collective-permute-start = (bf16[1,64,768]{2,1,0:T(8,128)(2,1)}, bf16[1,64,768]{2,1,0:T(8,128)(2,1)}, u32[]{:S(2)}, u32[]{:S(2)}) collective-permute-start(bf16[1,64,768]{2,1,0:T(8,128)(2,1)} %get-tuple-element.1297), channel_id=1, source_target_pairs={{0,16},{1,17},{2,18},{3,19},{4,20},{5,21},{6,22},{7,23},{8,24},{9,... | collective-permute-start | bytes 294920 | tf_op jit(solution)/shard_map/ppermute | solution.py:19
  135.4 20.8 %collective-permute-start.2 = (bf16[1,64,768]{2,1,0:T(8,128)(2,1)S(1)}, bf16[1,64,768]{2,1,0:T(8,128)(2,1)S(1)}, u32[]{:S(2)}, u32[]{:S(2)}) collective-permute-start(bf16[1,64,768]{2,1,0:T(8,128)(2,1)S(1)} %get-tuple-element.1301), channel_id=1, source_target_pairs={{0,16},{1,17},{2,18},{3,19},{4,20},{5,21},{6,22},{7,23},{8,24},{9,... | collective-permute-start | bytes 294920 | tf_op jit(solution)/shard_map/ppermute | solution.py:19
  188.3 26.3 %collective-permute-start.4 = (bf16[1,64,768]{2,1,0:T(8,128)(2,1)S(1)}, bf16[1,64,768]{2,1,0:T(8,128)(2,1)S(1)}, u32[]{:S(2)}, u32[]{:S(2)}) collective-permute-start(bf16[1,64,768]{2,1,0:T(8,128)(2,1)S(1)} %get-tuple-element.1305), channel_id=1, source_target_pairs={{0,16},{1,17},{2,18},{3,19},{4,20},{5,21},{6,22},{7,23},{8,24},{9,... | collective-permute-start | bytes 294920 | tf_op jit(solution)/shard_map/ppermute | solution.py:19
  246.5 26.5 %collective-permute-start.6 = (bf16[1,64,768]{2,1,0:T(8,128)(2,1)S(1)}, bf16[1,64,768]{2,1,0:T(8,128)(2,1)S(1)}, u32[]{:S(2)}, u32[]{:S(2)}) collective-permute-start(bf16[1,64,768]{2,1,0:T(8,128)(2,1)S(1)} %get-tuple-element.1309), channel_id=1, source_target_pairs={{0,16},{1,17},{2,18},{3,19},{4,20},{5,21},{6,22},{7,23},{8,24},{9,... | collective-permute-start | bytes 294920 | tf_op jit(solution)/shard_map/ppermute | solution.py:19
  354.0 57.3 %collective-permute-done.8 = bf16[1,64,768]{2,1,0:T(8,128)(2,1)S(1)} collective-permute-done((bf16[1,64,768]{2,1,0:T(8,128)(2,1)S(1)}, bf16[1,64,768]{2,1,0:T(8,128)(2,1)S(1)}, u32[]{:S(2)}, u32[]{:S(2)}) %collective-permute-start.8) | collective-permute-done | bytes 98336 | tf_op jit(solution)/shard_map/ppermute | solution.py:19
  463.6 32.4 %collective-permute-done.9 = bf16[1,64,768]{2,1,0:T(8,128)(2,1)S(1)} collective-permute-done((bf16[1,64,768]{2,1,0:T(8,128)(2,1)S(1)}, bf16[1,64,768]{2,1,0:T(8,128)(2,1)S(1)}, u32[]{:S(2)}, u32[]{:S(2)}) %collective-permute-start.9) | collective-permute-done | bytes 98336 | tf_op jit(solution)/shard_map/ppermute | solution.py:19
  547.8 32.5 %collective-permute-done.10 = bf16[1,64,768]{2,1,0:T(8,128)(2,1)S(1)} collective-permute-done((bf16[1,64,768]{2,1,0:T(8,128)(2,1)S(1)}, bf16[1,64,768]{2,1,0:T(8,128)(2,1)S(1)}, u32[]{:S(2)}, u32[]{:S(2)}) %collective-permute-start.10) | collective-permute-done | bytes 98336 | tf_op jit(solution)/shard_map/ppermute | solution.py:19
  632.3 32.3 %collective-permute-done.11 = bf16[1,64,768]{2,1,0:T(8,128)(2,1)S(1)} collective-permute-done((bf16[1,64,768]{2,1,0:T(8,128)(2,1)S(1)}, bf16[1,64,768]{2,1,0:T(8,128)(2,1)S(1)}, u32[]{:S(2)}, u32[]{:S(2)}) %collective-permute-start.11) | collective-permute-done | bytes 98336 | tf_op jit(solution)/shard_map/ppermute | solution.py:19
  823.8 29.0 %reduce-scatter.48.cloned.1.call-done = f32[48,768]{1,0:T(8,128)} async-done(((f32[768,768]{1,0:T(8,128)}), f32[48,768]{1,0:T(8,128)}) %reduce-scatter.48.cloned.1.call-update) | async-done | bytes 147472 | tf_op jit(solution)/shard_map/reduce_scatter | solution.py:391
  854.3 64.3 %reduce-scatter.46.cloned.1.call-done = f32[48,768]{1,0:T(8,128)} async-done(((f32[768,768]{1,0:T(8,128)}), f32[48,768]{1,0:T(8,128)}) %reduce-scatter.46.cloned.1.call-update) | async-done | bytes 147472 | tf_op jit(solution)/shard_map/reduce_scatter | solution.py:391
  920.2 64.6 %reduce-scatter.44.cloned.1.call-done = f32[48,768]{1,0:T(8,128)} async-done(((f32[768,768]{1,0:T(8,128)}), f32[48,768]{1,0:T(8,128)}) %reduce-scatter.44.cloned.1.call-update) | async-done | bytes 147472 | tf_op jit(solution)/shard_map/reduce_scatter | solution.py:391
  1042.2 18.3 add_bitcast_fusion.5
  1086.1 17.5 add_bitcast_fusion.6
  1135.5 57.7 %all-reduce.7 = (bf16[768]{0:T(1024)(128)(2,1)}, bf16[768]{0:T(1024)(128)(2,1)}, bf16[768]{0:T(1024)(128)(2,1)}, bf16[768]{0:T(1024)(128)(2,1)}, bf16[768]{0:T(1024)(128)(2,1)}) all-reduce(f32[768]{0:T(1024)} %multiply_add_fusion.11, f32[768]{0:T(1024)} %multiply_add_fusion.10, ...), channel_id=15, replica_groups=mesh['section'=2,'dp'=16] {'dp'}, use_global_device_ids=true, to_apply=%region_193.194.clone | all-reduce | flops 3840 | bytes 23040
  1222.1 53.7 %reduce-scatter.58.cloned.1.call-done = f32[48,1]{1,0:T(8,128)} async-done(((f32[768,1]{1,0:T(8,128)}), f32[48,1]{1,0:T(8,128)}) %reduce-scatter.58.cloned.1.call-update) | async-done | bytes 208
  1277.2 57.1 %reduce-scatter.56.cloned.1.call-done = f32[48,1]{1,0:T(8,128)} async-done(((f32[768,1]{1,0:T(8,128)}), f32[48,1]{1,0:T(8,128)}) %reduce-scatter.56.cloned.1.call-update) | async-done | bytes 208
  1335.6 56.7 %reduce-scatter.54.cloned.1.call-done = f32[48,1]{1,0:T(8,128)} async-done(((f32[768,1]{1,0:T(8,128)}), f32[48,1]{1,0:T(8,128)}) %reduce-scatter.54.cloned.1.call-update) | async-done | bytes 208
  1393.6 57.1 %reduce-scatter.52.cloned.1.call-done = f32[48,1]{1,0:T(8,128)} async-done(((f32[768,1]{1,0:T(8,128)}), f32[48,1]{1,0:T(8,128)}) %reduce-scatter.52.cloned.1.call-update) | async-done | bytes 208
  1452.0 60.8 %reduce-scatter.66.cloned.1.call-done = f32[192,1]{1,0:T(8,128)} async-done(((f32[3072,1]{1,0:T(8,128)}), f32[192,1]{1,0:T(8,128)}) %reduce-scatter.66.cloned.1.call-update) | async-done | bytes 784
  1516.2 22.3 %all-reduce.12.cloned.1.call-done = (bf16[48,768]{1,0:T(8,128)(2,1)}, bf16[48,768]{1,0:T(8,128)(2,1)}, bf16[48,768]{1,0:T(8,128)(2,1)}, bf16[48,768]{1,0:T(8,128)(2,1)}) async-done(((bf16[48,768]{1,0:T(8,128)(2,1)}, bf16[48,768]{1,0:T(8,128)(2,1)}, bf16[48,768]{1,0:T(8,128)(2,1)}, bf16[48,768]{1,0:T(8,128)(2,1)}), (bf16[48,768]{1,0:T(8,128)(2,1)}, bf16[48,768]{1,0:T(8,128)(2,1)}, bf16[48,768]{1,0:T(8,128)(2,1)}, ...) | async-done | bytes 294928 | tf_op jit(solution)/shard_map/psum | solution.py:393
  1544.8 61.4 %reduce-scatter.38.cloned.1.call-done = f32[1,48,768]{2,1,0:T(8,128)} async-done(((f32[1,768,768]{2,1,0:T(8,128)}), f32[1,48,768]{2,1,0:T(8,128)}) %reduce-scatter.38.cloned.1.call-update) | async-done | bytes 147472 | tf_op jit(solution)/shard_map/reduce_scatter | solution.py:388
  1606.2 93.5 %reduce-scatter.36.cloned.1.call-done = f32[1,48,2304]{2,1,0:T(8,128)} async-done(((f32[1,768,2304]{2,1,0:T(8,128)}), f32[1,48,2304]{2,1,0:T(8,128)}) %reduce-scatter.36.cloned.1.call-update) | async-done | bytes 442384 | tf_op jit(solution)/shard_map/reduce_scatter | solution.py:388
  1699.7 116.0 %reduce-scatter.42.cloned.1.call-done = f32[1,192,768]{2,1,0:T(8,128)} async-done(((f32[1,3072,768]{2,1,0:T(8,128)}), f32[1,192,768]{2,1,0:T(8,128)}) %reduce-scatter.42.cloned.1.call-update) | async-done | bytes 589840 | tf_op jit(solution)/shard_map/reduce_scatter | solution.py:388
  1815.7 115.7 %reduce-scatter.40.cloned.1.call-done = f32[1,48,3072]{2,1,0:T(8,128)} async-done(((f32[1,768,3072]{2,1,0:T(8,128)}), f32[1,48,3072]{2,1,0:T(8,128)}) %reduce-scatter.40.cloned.1.call-update) | async-done | bytes 589840 | tf_op jit(solution)/shard_map/reduce_scatter | solution.py:388
  (976 shorter events, 796.0 us)
Async XLA Ops:
  7.2 815.0 %reduce-scatter.50.cloned.1.call-start = ((), (), s32[]{:S(2)}) async-start(), calls=%async_computation.24 | async-start | bytes 2506752 | tf_op jit(solution)/shard_map/reduce_scatter | solution.py:391
  9.7 106.6 %collective-permute-start.1 = (bf16[1,128,768]{2,1,0:T(8,128)(2,1)}, bf16[1,128,768]{2,1,0:T(8,128)(2,1)}, u32[]{:S(2)}, u32[]{:S(2)}) collective-permute-start(bf16[1,128,768]{2,1,0:T(8,128)(2,1)} %get-tuple-element.1267), channel_id=1, source_target_pairs={{0,16},{1,17},{2,18},{3,19},{4,20},{5,21},{6,22},{7,23},{8,24},{9,... | collective-permute-start | bytes 589832 | tf_op jit(solution)/shard_map/ppermute | solution.py:19
  86.1 70.0 %collective-permute-start.3 = (bf16[1,128,768]{2,1,0:T(8,128)(2,1)}, bf16[1,128,768]{2,1,0:T(8,128)(2,1)}, u32[]{:S(2)}, u32[]{:S(2)}) collective-permute-start(bf16[1,128,768]{2,1,0:T(8,128)(2,1)} %get-tuple-element.1266), channel_id=1, source_target_pairs={{0,16},{1,17},{2,18},{3,19},{4,20},{5,21},{6,22},{7,23},{8,24},{9,... | collective-permute-start | bytes 589832 | tf_op jit(solution)/shard_map/ppermute | solution.py:19
  88.1 126.5 %collective-permute-start.5 = (bf16[1,128,768]{2,1,0:T(8,128)(2,1)}, bf16[1,128,768]{2,1,0:T(8,128)(2,1)}, u32[]{:S(2)}, u32[]{:S(2)}) collective-permute-start(bf16[1,128,768]{2,1,0:T(8,128)(2,1)} %get-tuple-element.1265), channel_id=1, source_target_pairs={{0,16},{1,17},{2,18},{3,19},{4,20},{5,21},{6,22},{7,23},{8,24},{9,... | collective-permute-start | bytes 589832 | tf_op jit(solution)/shard_map/ppermute | solution.py:19
  90.1 183.0 %collective-permute-start.7 = (bf16[1,128,768]{2,1,0:T(8,128)(2,1)}, bf16[1,128,768]{2,1,0:T(8,128)(2,1)}, u32[]{:S(2)}, u32[]{:S(2)}) collective-permute-start(bf16[1,128,768]{2,1,0:T(8,128)(2,1)} %get-tuple-element.1268), channel_id=1, source_target_pairs={{0,16},{1,17},{2,18},{3,19},{4,20},{5,21},{6,22},{7,23},{8,24},{9,... | collective-permute-start | bytes 589832 | tf_op jit(solution)/shard_map/ppermute | solution.py:19
  694.1 158.7 %reduce-scatter.48.cloned.1.call-start = ((), (), s32[]{:S(2)}) async-start(), calls=%async_computation.23 | async-start | bytes 2506752 | tf_op jit(solution)/shard_map/reduce_scatter | solution.py:391
  716.3 202.3 %reduce-scatter.46.cloned.1.call-start = ((), (), s32[]{:S(2)}) async-start(), calls=%async_computation.22 | async-start | bytes 2506752 | tf_op jit(solution)/shard_map/reduce_scatter | solution.py:391
  738.8 246.0 %reduce-scatter.44.cloned.1.call-start = ((), (), s32[]{:S(2)}) async-start(), calls=%async_computation.21 | async-start | bytes 2506752 | tf_op jit(solution)/shard_map/reduce_scatter | solution.py:391
  761.1 455.7 %reduce-scatter.68.cloned.1.call-start = ((), (), s32[]{:S(2)}) async-start(), calls=%async_computation.33 | async-start | bytes 417792
  785.0 433.1 %reduce-scatter.64.cloned.1.call-start = ((), (), s32[]{:S(2)}) async-start(), calls=%async_computation.31 | async-start | bytes 417792
  786.8 432.7 %reduce-scatter.62.cloned.1.call-start = ((), (), s32[]{:S(2)}) async-start(), calls=%async_computation.30 | async-start | bytes 417792
  788.4 432.4 %reduce-scatter.60.cloned.1.call-start = ((), (), s32[]{:S(2)}) async-start(), calls=%async_computation.29 | async-start | bytes 417792
  790.1 485.7 %reduce-scatter.58.cloned.1.call-start = ((), (), s32[]{:S(2)}) async-start(), calls=%async_computation.28 | async-start | bytes 417792
  805.9 528.3 %reduce-scatter.56.cloned.1.call-start = ((), (), s32[]{:S(2)}) async-start(), calls=%async_computation.27 | async-start | bytes 417792
  812.1 580.2 %reduce-scatter.54.cloned.1.call-start = ((), (), s32[]{:S(2)}) async-start(), calls=%async_computation.26 | async-start | bytes 417792
  813.8 636.9 %reduce-scatter.52.cloned.1.call-start = ((), (), s32[]{:S(2)}) async-start(), calls=%async_computation.25 | async-start | bytes 417792
  815.5 697.3 %reduce-scatter.66.cloned.1.call-start = ((), (), s32[]{:S(2)}) async-start(), calls=%async_computation.32 | async-start | bytes 1671168
  819.3 719.2 %all-reduce.12.cloned.1.call-start = ((), (), s32[]{:S(2)}) async-start(), calls=%async_computation.34 | async-start | bytes 589824 | tf_op jit(solution)/shard_map/psum | solution.py:393
  986.3 619.9 %reduce-scatter.38.cloned.1.call-start = ((), (), s32[]{:S(2)}) async-start(), calls=%async_computation.18 | async-start | bytes 2506752 | tf_op jit(solution)/shard_map/reduce_scatter | solution.py:388
  992.5 707.2 %reduce-scatter.36.cloned.1.call-start = ((), (), s32[]{:S(2)}) async-start(), calls=%async_computation.17 | async-start | bytes 7520256 | tf_op jit(solution)/shard_map/reduce_scatter | solution.py:388
  1013.9 801.8 %reduce-scatter.42.cloned.1.call-start = ((), (), s32[]{:S(2)}) async-start(), calls=%async_computation.20 | async-start | bytes 10027008 | tf_op jit(solution)/shard_map/reduce_scatter | solution.py:388
  1060.6 870.7 %reduce-scatter.40.cloned.1.call-start = ((), (), s32[]{:S(2)}) async-start(), calls=%async_computation.19 | async-start | bytes 10027008 | tf_op jit(solution)/shard_map/reduce_scatter | solution.py:388
  1120.5 92.3 %collective-permute-start.14 = (bf16[1,128,768]{2,1,0:T(8,128)(2,1)}, bf16[1,128,768]{2,1,0:T(8,128)(2,1)}, u32[]{:S(2)}, u32[]{:S(2)}) collective-permute-start(bf16[1,128,768]{2,1,0:T(8,128)(2,1)} %slice.292), channel_id=1, source_target_pairs={{16,0},{17,1},{18,2},{19,3},{20,4},{21,5},{22,6},{23,7},{24,8},{25... | collective-permute-start | bytes 589832 | tf_op jit(solution)/shard_map/ppermute | solution.py:19
  1125.4 388.9 %collective-permute-start.15 = (bf16[1,128,768]{2,1,0:T(8,128)(2,1)}, bf16[1,128,768]{2,1,0:T(8,128)(2,1)}, u32[]{:S(2)}, u32[]{:S(2)}) collective-permute-start(bf16[1,128,768]{2,1,0:T(8,128)(2,1)} %slice.291), channel_id=1, source_target_pairs={{16,0},{17,1},{18,2},{19,3},{20,4},{21,5},{22,6},{23,7},{24,8},{25... | collective-permute-start | bytes 589832 | tf_op jit(solution)/shard_map/ppermute | solution.py:19
  (234 other events, 2329.3 us)
Sparse Core Ops, SparseCore 0:
  694.2 92.2 reduce-scatter.49
  790.8 61.9 reduce-scatter.47
  856.6 62.0 reduce-scatter.45
  922.7 61.9 reduce-scatter.43
  988.1 54.5 reduce-scatter.67
  1046.4 54.6 reduce-scatter.63
  1104.6 54.5 reduce-scatter.61
  1163.1 54.5 reduce-scatter.59
  1221.3 54.5 reduce-scatter.57
  1279.6 54.5 reduce-scatter.55
  1337.7 54.5 reduce-scatter.53
  1396.1 54.6 reduce-scatter.51
  1454.4 58.3 reduce-scatter.65
  1515.3 23.2 all-reduce.11
  1543.2 62.9 reduce-scatter.37
  1610.7 88.9 reduce-scatter.35
  1704.8 110.8 reduce-scatter.41
  1820.2 111.0 reduce-scatter.39
where the time goes:
time: 1960 us; the launch traced here: 1940 us
  waiting for transfers between devices  1010 us (52%)
  matrix products  297 us (15%)
  local copies, waits for them, and re-layouts  262 us (13%)
  other arithmetic  166 us (8%)
  starting transfers between devices  120 us (6%)
  blocking collectives  65.4 us (3%)
    reduce_scatter x4, waiting for transfers between devices, body(): lax.psum_scatter(tuple((total[None] for total in layer_sums)), 'dp', scat...  387 us
    unnamed x27, waiting for transfers between devices  286 us
    reduce_scatter x4, waiting for transfers between devices, body(): lax.psum_scatter(cross_sums, 'dp', scatter_dimension=0, tiled=True)  158 us
    ppermute x16, waiting for transfers between devices, shifted(): return lax.ppermute(block, axis, route)  156 us
    dot_general x20, matrix products, weight_product(): jnp.einsum('bsi,bsj->ij', rows, grad, preferred_element_type=jnp.float32)  126 us
    ppermute x16, starting transfers between devices, shifted(): return lax.ppermute(block, axis, route)  119 us
    another operation x104, local copies, waits for them, and re-layouts  107 us
    dot_general x20, matrix products, back_product(): jnp.einsum('bsj,ij->bsi', grad, weight, preferred_element_type=jnp.float32)  73.2 us
  transfers between devices with their start and end apart: 34, of which 20 were waited for; matrix products, arithmetic and copies ran while one was open for 24% of the time, Pallas kernels for 0%

commit v1 on v0

--- a/solution.py
+++ b/solution.py
@@ -1,12 +1,18 @@
 import jax
 import jax.numpy as jnp
 from jax import lax
+from jax.experimental import pallas as pl
+from jax.experimental.pallas import tpu as pltpu
 from jax.sharding import PartitionSpec as P
 
 HEADS = 12
 HEAD_DIM = 64
-MB_CAPS = 1
-MICRO = 4
+MB_CAPS = 4
+MICRO = 1
+ROWS = 48
+CHUNKS = 16
+SHARED_CHUNKS = 12
+VECTORS = 24
 
 
 EPS = 1e-05
@@ -210,6 +216,174 @@
     dhidden, gain_grad, shift_grad = norm_back(dentry, normed, inverse, cross[0])
     parts = (gain_grad, shift_grad, query_grad, column_sum(dquery), out_grad, out_bias_grad)
     return (grad + dhidden, parts, jnp.concatenate([dkeys, dvalues], -1))
+
+
+def select_bit(rank, axes, bit, value):
+    return tuple(value if axis == bit else slice(None) for axis in axes)
+
+
+def add_blocks(into, term, count):
+    lead = into.shape[:-2]
+
+    def place(i):
+        where = []
+        for size in reversed(lead):
+            where.append(lax.rem(i, size))
+            i = lax.div(i, size)
+        return tuple(reversed(where))
+
+    if not lead:
+        into[...] = into[...] + term[...]
+        return
+
+    @pl.loop(0, count)
+    def _(i):
+        into[place(i)] = into[place(i)] + term[place(i)]
+
+
+def scatter_kernel(blocks, vectors, shards, totals, grads, *scratch):
+    halves = scratch[:4]
+    landed, load_sem, send_sem, recv_sem, vsend_sem, vrecv_sem = scratch[4:]
+    section = lax.axis_index("section")
+    dp = lax.axis_index("dp")
+    bits = [lax.rem(lax.div(dp, 1 << k), 2) for k in range(4)]
+    partners = [dp + (1 << k) * (1 - 2 * bits[k]) for k in range(4)]
+    count = jnp.where(section == 1, CHUNKS, SHARED_CHUNKS)
+
+    barrier = pltpu.get_barrier_semaphore()
+    for partner in partners:
+        pl.semaphore_signal(
+            barrier, inc=1, device_id={"dp": partner}, device_id_type=pl.DeviceIdType.MESH
+        )
+    pl.semaphore_wait(barrier, 4)
+
+    def step(chunk, k):
+        axes = tuple(range(3, k - 1, -1))
+        source = (grads if k == 0 else halves[k - 1]).at[chunk]
+        send = source.at[select_bit(4, axes, k, 1 - bits[k])]
+        keep = source.at[select_bit(4, axes, k, bits[k])]
+        into = halves[k].at[chunk]
+        copy = pltpu.make_async_remote_copy(
+            src_ref=send,
+            dst_ref=into,
+            send_sem=send_sem.at[chunk, k],
+            recv_sem=recv_sem.at[chunk, k],
+            device_id={"dp": partners[k]},
+            device_id_type=pl.DeviceIdType.MESH,
+        )
+        return copy, into, keep
+
+    def load(chunk):
+        return pltpu.make_async_copy(blocks.at[chunk], grads.at[chunk], load_sem.at[chunk])
+
+    @pl.loop(0, count)
+    def _(chunk):
+        load(chunk).start()
+
+    @pl.loop(0, count)
+    def _(chunk):
+        load(chunk).wait()
+        step(chunk, 0)[0].start()
+
+    totals[...] = vectors[...]
+    for k in range(4):
+        copy = pltpu.make_async_remote_copy(
+            src_ref=totals,
+            dst_ref=landed.at[k],
+            send_sem=vsend_sem.at[k],
+            recv_sem=vrecv_sem.at[k],
+            device_id={"dp": partners[k]},
+            device_id_type=pl.DeviceIdType.MESH,
+        )
+        copy.start()
+        copy.wait()
+        totals[...] = totals[...] + landed[k]
+
+    @pl.loop(0, count + 3)
+    def _(tick):
+        for k in range(4):
+            chunk = tick - k
+
+            @pl.when((chunk >= 0) & (chunk < count))
+            def _():
+                copy, into, keep = step(chunk, k)
+                copy.wait()
+                add_blocks(into, keep, 8 >> k)
+                if k < 3:
+                    step(chunk, k + 1)[0].start()
+                else:
+                    shards[chunk] = into[...]
+
+
+def scatter(blocks, vectors):
+    lead = (2, 2, 2, 2)
+    tail = blocks.shape[2:]
+    blocks = blocks.reshape((CHUNKS,) + lead + tail)
+    buffers = [pltpu.VMEM((CHUNKS,) + lead[k:] + tail, jnp.bfloat16) for k in range(5)]
+    return pl.pallas_call(
+        scatter_kernel,
+        out_shape=(
+            jax.ShapeDtypeStruct((CHUNKS,) + tail, jnp.bfloat16),
+            jax.ShapeDtypeStruct(vectors.shape, jnp.float32),
+        ),
+        in_specs=[pl.BlockSpec(memory_space=pl.ANY), pl.BlockSpec(memory_space=pltpu.VMEM)],
+        out_specs=[pl.BlockSpec(memory_space=pltpu.VMEM)] * 2,
+        scratch_shapes=buffers
+        + [pltpu.VMEM((4,) + vectors.shape, jnp.float32)]
+        + [pltpu.SemaphoreType.DMA((CHUNKS,))]
+        + [pltpu.SemaphoreType.DMA((CHUNKS, 4))] * 2
+        + [pltpu.SemaphoreType.DMA((4,))] * 2,
+        compiler_params=pltpu.CompilerParams(
+            collective_id=0, has_side_effects=True, vmem_limit_bytes=60 * 2**20
+        ),
+        name="scatter",
+    )(blocks, vectors)
+
+
+def reduce_fast(layer_sums, cross_sums, section_index):
+    gain, shift, packed, query_b, value_b, out_w, out_b, fgain, fshift, exp_w, exp_b, red_w, red_b = layer_sums
+    cgain, cshift, cquery, cquery_b, ckey, cvalue, cvalue_b, cout, cout_b = cross_sums
+    n = lax.axis_size("dp")
+    width = cquery.shape[0]
+
+    def columns(weight):
+        parts = weight.shape[1] // width
+        return weight.reshape(n, ROWS, parts, width).transpose(2, 0, 1, 3)
+
+    chunks = [red_w.reshape(n, 4, ROWS, width).transpose(1, 0, 2, 3), columns(exp_w)]
+    chunks += [columns(out_w), columns(packed)]
+    chunks += [columns(w) for w in (cquery, ckey, cvalue, cout)]
+    blocks = jnp.concatenate([c.astype(jnp.bfloat16) for c in chunks], 0)
+    vectors = [gain, shift, query_b, value_b, out_b, fgain, fshift, red_b]
+    vectors = [v[None] for v in vectors] + [exp_b.reshape(4, width)]
+    vectors += [v[None] for v in (cgain, cshift, cquery_b, cvalue_b, cout_b)]
+    vectors = jnp.concatenate(vectors + [jnp.zeros((VECTORS - 17, width), jnp.float32)], 0)
+    shards, totals = scatter(blocks, vectors)
+    from_two = [(1, 0)]
+    is_two = section_index == 1
+    cross_shards = shards[12:]
+    cross_shards = jnp.where(is_two, cross_shards, lax.ppermute(cross_shards, "section", from_two))
+    cross_totals = totals[12:17]
+    cross_totals = jnp.where(is_two, cross_totals, lax.ppermute(cross_totals, "section", from_two))
+    shards = shards.astype(jnp.float32)
+    cross_shards = cross_shards.astype(jnp.float32)
+    dp = lax.axis_index("dp")
+    own = lax.dynamic_slice_in_dim(totals[:8], dp * ROWS, ROWS, 1)
+    own_exp = lax.dynamic_slice_in_dim(totals[8:12].reshape(-1), dp * 4 * ROWS, 4 * ROWS, 0)
+    own_cross = lax.dynamic_slice_in_dim(cross_totals, dp * ROWS, ROWS, 1)
+
+    def joined(parts):
+        return parts.transpose(1, 0, 2).reshape(ROWS, -1)
+
+    layer = (
+        own[0], own[1], joined(shards[9:12]), own[2], own[3], shards[8], own[4], own[5], own[6],
+        joined(shards[4:8]), own_exp, shards[:4].reshape(4 * ROWS, width), own[7],
+    )
+    crossed = (
+        own_cross[0], own_cross[1], cross_shards[0], own_cross[2], cross_shards[1], cross_shards[2],
+        own_cross[3], cross_shards[3], own_cross[4],
+    )
+    return tuple(part[None] for part in layer), crossed
 
 
 def body(
@@ -385,13 +559,16 @@
             coming = shifted(image_part[:, :half].astype(jnp.bfloat16), "section", -1).astype(
                 jnp.float32
             )
-    shared = lax.psum_scatter(
-        tuple((total[None] for total in layer_sums)), "dp", scatter_dimension=1, tiled=True
-    )
-    scattered = lax.psum_scatter(cross_sums, "dp", scatter_dimension=0, tiled=True)
-    crossed = jax.tree.map(
-        lambda part: part.astype(jnp.float32), lax.psum(for_sending(tuple(scattered)), "section")
-    )
+    if lax.axis_size("dp") == 16:
+        shared, crossed = reduce_fast(layer_sums, cross_sums, section_index)
+    else:
+        shared = lax.psum_scatter(
+            tuple((total[None] for total in layer_sums)), "dp", scatter_dimension=1, tiled=True
+        )
+        scattered = lax.psum_scatter(cross_sums, "dp", scatter_dimension=0, tiled=True)
+        crossed = jax.tree.map(
+            lambda part: part.astype(jnp.float32), lax.psum(for_sending(tuple(scattered)), "section")
+        )
     return (finished[None], input_grads[None], image_grads) + tuple(shared) + tuple(crossed)
 
 

time: 1960 us -> 735 us (0.38)
  the two profiles are of different devices: /device:TPU:0 before, /device:TPU:14 now
where the time goes in v1:
time: 735 us; the launch traced here: 725 us
  local copies, waits for them, and re-layouts  242 us (33%)
  matrix products  212 us (29%)
  Pallas kernels  144 us (20%)
  other arithmetic  96.7 us (13%)
  waiting for transfers between devices  13.7 us (2%)
  starting transfers between devices  10.9 us (1%)
    pallas_call x1, Pallas kernels, scatter(): pl.pallas_call(scatter_kernel, out_shape=(jax.ShapeDtypeStruct((CHUNKS,)...  144 us
    dot_general x14, matrix products, weight_product(): jnp.einsum('bsi,bsj->ij', rows, grad, preferred_element_type=jnp.float32)  63.7 us
    dot_general x14, matrix products, back_product(): jnp.einsum('bsj,ij->bsi', grad, weight, preferred_element_type=jnp.float32)  48.3 us
    dot_general x14, matrix products, product(): jnp.einsum('bsi,ij->bsj', rows, weight, preferred_element_type=jnp.float32)  43 us
    reshape x12, local copies, waits for them, and re-layouts, split_heads(): return rows.reshape(rows.shape[0], rows.shape[1], HEADS, HEAD_DIM)  28.3 us
    convert_element_type x5, local copies, waits for them, and re-layouts, reduce_fast(): blocks = jnp.concatenate([c.astype(jnp.bfloat16) for c in chunks], 0)  26.9 us
    unnamed x277, local copies, waits for them, and re-layouts  26 us
    convert_element_type x8, local copies, waits for them, and re-layouts, attend_back(): dquery.reshape(query.shape).astype(jnp.bfloat16)  19.9 us
  transfers between devices with their start and end apart: 6, of which 2 were waited for; matrix products, arithmetic and copies ran while one was open for 37% of the time, Pallas kernels for 20%

profile of v1, /device:TPU:14, one launch (start us, length us, event | category | flops | bytes accessed | tf_op | source)
XLA Modules:
  0.0 724.9 jit_solution(2835569812950236685)
XLA Ops:
  30.2 38.6 %conditional.4 = (f32[4,64,768]{2,1,0:T(8,128)}, f32[4,64,768]{2,1,0:T(8,128)}, f32[4,64,1]{1,0,2:T(4,128)}, bf16[4,64,768]{2,1,0:T(8,128)(2,1)}, bf16[4,64,768]...) conditional(s32[]{:T(128)} %convert_element_type.529, ...), branch_computations={%region_4.5_spmd, %region_5.10_spmd} | conditional | flops 3234198784 | bytes 60006608 | solution.py:509
  72.8 5.1 fusion.214
  78.0 7.1 fusion.108
  93.2 10.2 %collective-permute-done = bf16[4,64,768]{2,1,0:T(8,128)(2,1)} collective-permute-done((bf16[4,64,768]{2,1,0:T(8,128)(2,1)}, bf16[4,64,768]{2,1,0:T(8,128)(2,1)}, u32[]{:S(2)}, u32[]{:S(2)}) %collective-permute-start) | collective-permute-done | bytes 393248 | tf_op jit(solution)/shard_map/ppermute | solution.py:25
  124.5 39.2 %conditional.5 = (f32[4,64,768]{2,1,0:T(8,128)}, f32[4,64,768]{2,1,0:T(8,128)}, f32[4,64,1]{1,0,2:T(4,128)}, bf16[4,64,768]{2,1,0:T(8,128)(2,1)}, bf16[4,64,768]...) conditional(s32[]{:T(128)} %convert_element_type.529, ...), branch_computations={%region_16.17_spmd, %region_17.22_spmd} | conditional | flops 3234198784 | bytes 60006608 | solution.py:509
  167.6 5.9 fusion.215
  173.6 6.0 convert_reduce_fusion.7
  186.0 63.2 %conditional.6 = (f32[4,64,768]{2,1,0:T(8,128)}, f32[768]{0:T(1024)}, f32[768]{0:T(1024)}, f32[768,768]{0,1:T(8,128)}, f32[768]{0:T(1024)}, /*index=5*/f32[768,7...) conditional(s32[]{:T(128)} %convert_element_type.529, ...), branch_computations={%region_26.27_spmd, %region_27.36_spmd} | conditional | flops 6573581312 | bytes 159750592 | solution.py:538
  228.0 7.0 fusion.24
  266.8 6.5 fusion.241
  273.3 7.1 fusion.111
  283.8 5.2 fusion.234
  326.9 5.8 fusion.238
  338.0 5.0 convert_reduce_fusion.6
  349.6 62.0 %conditional.7 = (f32[4,64,768]{2,1,0:T(8,128)}, f32[768]{0:T(1024)}, f32[768]{0:T(1024)}, f32[768,768]{0,1:T(8,128)}, f32[768]{0:T(1024)S(1)}, /*index=5*/f32[7...) conditional(s32[]{:T(128)} %convert_element_type.529, ...), branch_computations={%region_41.42_spmd, %region_42.51_spmd} | conditional | flops 5362476032 | bytes 158190048 | solution.py:538
  386.2 5.6 convolution_bitcast_fusion.3
  393.1 4.9 fusion.254
  478.1 6.5 fusion.63
  484.6 8.8 %convert_element_type.605 = bf16[16,48,3,768]{3,2,1,0:T(4,128)(2,1)} reshape(bf16[768,2304]{1,0:T(8,128)(2,1)} %fusion.63) | data formatting | bytes 7077888 | tf_op jit(solution)/shard_map/convert_element_type | solution.py:356
  493.4 4.8 copy.178
  498.2 7.8 %fusion.59 = bf16[768,3072]{1,0:T(8,128)(2,1)} fusion(f32[768,3072,1]{1,0,2:T(8,128)} %fusion.241, bf16[4,64,3072]{2,1,0:T(8,128)(2,1)S(1)} %copy-done.156, f32[]{:T(128)S(6)} %convert_element_type.552, f32[]{:T(128)S(6)} %convert_element_type.592, f32[4,64,768]{2,1,0:T(8,128)} %get-tuple-element.208, f32[768]{0:T(1024)S(1)} %copy-done.152, ...), kind=kOutput, calls=%fused_computation.121 | convolution fusion | flops 1218379776 | bytes 16523272 | tf_op jit(solution)/shard_map/bsi,bsj->ij/dot_general | solution.py:59
  506.0 9.8 %convert_element_type.600 = bf16[16,48,4,768]{3,2,1,0:T(4,128)(2,1)} reshape(bf16[768,3072]{1,0:T(8,128)(2,1)} %fusion.59) | data formatting | bytes 9437184 | tf_op jit(solution)/shard_map/convert_element_type | solution.py:356
  518.9 5.3 fusion.61
  550.0 144.4 %scatter.1 = (bf16[16,48,768]{2,1,0:T(8,128)(2,1)}, f32[24,768]{1,0:T(8,128)}) custom-call(bf16[16,2,2,2,2,48,768]{6,5,4,3,2,1,0:T(8,128)(2,1)} %constant_dynamic-update-slice_fusion.10.blocks, f32[24,768]{1,0:T(8,128)} %concatenate.47.vectors), custom_call_target="tpu_custom_call" | custom-call | tf_op jit(solution)/shard_map/scatter/pallas_call | solution.py:323
  (598 shorter events, 451.6 us)
Async XLA Ops:
  0.7 10.9 %copy-start = (bf16[1,768,2304]{2,1,0:T(8,128)(2,1)S(1)}, bf16[1,768,2304]{2,1,0:T(8,128)(2,1)}, u32[]{:S(2)}) copy-start(bf16[1,768,2304]{2,1,0:T(8,128)(2,1)} %param.40) | copy-start | bytes 10616836
  5.0 67.8 %copy-start.103 = (f32[768]{0:T(1024)}, f32[768]{0:T(1024)S(1)}, u32[]{:S(2)}) copy-start(f32[768]{0:T(1024)S(1)} %reduce.21) | copy-start | bytes 9220
  15.2 8.6 %copy-start.148 = (f32[768]{0:T(1024)S(1)}, f32[768]{0:T(1024)}, u32[]{:S(2)}) copy-start(f32[768]{0:T(1024)} %param.57) | copy-start | bytes 9220
  72.8 12.3 %slice-start = ((s8[4718592]{0:T(1024)(128)(4,1)}), s8[4194304]{0:T(1024)(128)(4,1)S(1)}, s32[]{:S(2)}) async-start(s8[4718592]{0:T(1024)(128)(4,1)} %bitcast.424), calls=%async_computation | async-start | bytes 8388608
  72.8 12.2 %slice-start.1 = ((s8[4718592]{0:T(1024)(128)(4,1)}), s8[524288]{0:T(1024)(128)(4,1)S(1)}, s32[]{:S(2)}) async-start(s8[4718592]{0:T(1024)(128)(4,1)} %bitcast.424), calls=%async_computation.1 | async-start | bytes 1048576
  78.0 11.0 %copy-start.51 = (f32[4,64,3072]{2,1,0:T(8,128)}, f32[4,64,3072]{2,1,0:T(8,128)S(1)}, u32[]{:S(2)}) copy-start(f32[4,64,3072]{2,1,0:T(8,128)S(1)} %get-tuple-element.483) | copy-start | bytes 9437188
  89.0 14.4 %collective-permute-start = (bf16[4,64,768]{2,1,0:T(8,128)(2,1)}, bf16[4,64,768]{2,1,0:T(8,128)(2,1)}, u32[]{:S(2)}, u32[]{:S(2)}) collective-permute-start(bf16[4,64,768]{2,1,0:T(8,128)(2,1)} %fusion.155), channel_id=1, source_target_pairs={{0,16},{1,17},{2,18},{3,19},{4,20},{5,21},{6,22},{7,23},{8,24},{9,... | collective-permute-start | bytes 1179656 | tf_op jit(solution)/shard_map/ppermute | solution.py:25
  90.4 30.5 %collective-permute-start.1 = (bf16[4,128,768]{2,1,0:T(8,128)(2,1)}, bf16[4,128,768]{2,1,0:T(8,128)(2,1)}, u32[]{:S(2)}, u32[]{:S(2)}) collective-permute-start(bf16[4,128,768]{2,1,0:T(8,128)(2,1)} %param.35), channel_id=1, source_target_pairs={{0,16},{1,17},{2,18},{3,19},{4,20},{5,21},{6,22},{7,23},{8,24},{9,... | collective-permute-start | bytes 2359304 | tf_op jit(solution)/shard_map/ppermute | solution.py:25
  166.2 17.4 %copy-start.125 = (f32[4,64]{1,0:T(4,128)}, f32[4,64]{1,0:T(4,128)S(1)}, u32[]{:S(2)}) copy-start(f32[4,64]{1,0:T(4,128)S(1)} %broadcast_multiply_fusion.14) | copy-start | bytes 3076
  167.6 16.0 %copy-start.141 = (f32[4,64]{1,0:T(4,128)}, f32[4,64]{1,0:T(4,128)S(1)}, u32[]{:S(2)}) copy-start(f32[4,64]{1,0:T(4,128)S(1)} %add_rsqrt_fusion.2) | copy-start | bytes 3076
  167.6 12.0 %slice-start.4 = ((s8[4718592]{0:T(1024)(128)(4,1)}), s8[4194304]{0:T(1024)(128)(4,1)S(1)}, s32[]{:S(2)}) async-start(s8[4718592]{0:T(1024)(128)(4,1)} %bitcast.428), calls=%async_computation.4 | async-start | bytes 8388608
  263.4 17.0 %slice-start.2 = ((s8[4718592]{0:T(1024)(128)(4,1)}), s8[4194304]{0:T(1024)(128)(4,1)S(1)}, s32[]{:S(2)}) async-start(s8[4718592]{0:T(1024)(128)(4,1)} %bitcast.426), calls=%async_computation.2 | async-start | bytes 8388608
  266.7 13.6 %slice-start.3 = ((s8[4718592]{0:T(1024)(128)(4,1)}), s8[524288]{0:T(1024)(128)(4,1)S(1)}, s32[]{:S(2)}) async-start(s8[4718592]{0:T(1024)(128)(4,1)} %bitcast.426), calls=%async_computation.3 | async-start | bytes 1048576
  311.1 410.2 %collective-permute-start.3 = (bf16[4,128,768]{2,1,0:T(8,128)(2,1)}, bf16[4,128,768]{2,1,0:T(8,128)(2,1)}, u32[]{:S(2)}, u32[]{:S(2)}) collective-permute-start(bf16[4,128,768]{2,1,0:T(8,128)(2,1)} %slice.234), channel_id=1, source_target_pairs={{16,0},{17,1},{18,2},{19,3},{20,4},{21,5},{22,6},{23,7},{24,8},{25... | collective-permute-start | bytes 2359304 | tf_op jit(solution)/shard_map/ppermute | solution.py:25
  318.7 17.5 %collective-permute-start.2 = (bf16[4,64,768]{2,1,0:T(8,128)(2,1)}, bf16[4,64,768]{2,1,0:T(8,128)(2,1)}, u32[]{:S(2)}, u32[]{:S(2)}) collective-permute-start(bf16[4,64,768]{2,1,0:T(8,128)(2,1)} %fusion.250), channel_id=1, source_target_pairs={{16,0},{17,1},{18,2},{19,3},{20,4},{21,5},{22,6},{23,7},{24,8},{25... | collective-permute-start | bytes 1179656 | tf_op jit(solution)/shard_map/ppermute | solution.py:25
  326.9 9.2 %copy-start.48 = (bf16[1,4,64,768]{3,2,1,0:T(8,128)(2,1)S(1)}, bf16[1,4,64,768]{3,2,1,0:T(8,128)(2,1)}, u32[]{:S(2)}) copy-start(bf16[1,4,64,768]{3,2,1,0:T(8,128)(2,1)} %param.37) | copy-start | bytes 1179652
  326.9 9.2 %copy-start.117 = (f32[4,64]{1,0:T(4,128)S(1)}, f32[4,64]{1,0:T(4,128)}, u32[]{:S(2)}) copy-start(f32[4,64]{1,0:T(4,128)} %get-tuple-element.479) | copy-start | bytes 3076
  326.9 11.1 %copy-start.52 = (f32[4,64,3072]{2,1,0:T(8,128)S(1)}, f32[4,64,3072]{2,1,0:T(8,128)}, u32[]{:S(2)}) copy-start(f32[4,64,3072]{2,1,0:T(8,128)} %copy-done.51) | copy-start | bytes 9437188
  326.9 16.1 %slice-start.6 = ((s8[4718592]{0:T(1024)(128)(4,1)}), s8[4194304]{0:T(1024)(128)(4,1)S(1)}, s32[]{:S(2)}) async-start(s8[4718592]{0:T(1024)(128)(4,1)} %bitcast.430), calls=%async_computation.6 | async-start | bytes 8388608
  332.7 10.3 %slice-start.7 = ((s8[4718592]{0:T(1024)(128)(4,1)}), s8[524288]{0:T(1024)(128)(4,1)S(1)}, s32[]{:S(2)}) async-start(s8[4718592]{0:T(1024)(128)(4,1)} %bitcast.430), calls=%async_computation.7 | async-start | bytes 1048576
  411.6 8.1 %copy-start.133 = (f32[768]{0:T(1024)}, f32[768]{0:T(1024)S(1)}, u32[]{:S(2)}) copy-start(f32[768]{0:T(1024)S(1)} %get-tuple-element.241) | copy-start | bytes 9220
  694.5 8.7 %copy-start.43 = (bf16[16,48,768]{2,1,0:T(8,128)(2,1)S(1)}, bf16[16,48,768]{2,1,0:T(8,128)(2,1)}, u32[]{:S(2)}) copy-start(bf16[16,48,768]{2,1,0:T(8,128)(2,1)} %get-tuple-element.247) | copy-start | bytes 3538948
  699.9 18.2 %collective-permute-start.4 = (f32[5,768]{1,0:T(8,128)}, f32[5,768]{1,0:T(8,128)}, u32[]{:S(2)}, u32[]{:S(2)}) collective-permute-start(f32[5,768]{1,0:T(8,128)} %slice.167), channel_id=1, source_target_pairs={{16,0},{17,1},{18,2},{19,3},{20,4},{21,5},{22,6},{23,7},{24,8},{25... | collective-permute-start | bytes 46088 | tf_op jit(solution)/shard_map/ppermute | solution.py:367
  706.0 13.4 %collective-permute-start.5 = (bf16[4,48,768]{2,1,0:T(8,128)(2,1)}, bf16[4,48,768]{2,1,0:T(8,128)(2,1)}, u32[]{:S(2)}, u32[]{:S(2)}) collective-permute-start(bf16[4,48,768]{2,1,0:T(8,128)(2,1)} %slice.170), channel_id=1, source_target_pairs={{16,0},{17,1},{18,2},{19,3},{20,4},{21,5},{22,6},{23,7},{24,8},{25... | collective-permute-start | bytes 884744 | tf_op jit(solution)/shard_map/ppermute | solution.py:365
  (149 other events, 544.6 us)

commit v2 on v0

--- a/solution.py
+++ b/solution.py
@@ -1,12 +1,14 @@
 import jax
 import jax.numpy as jnp
 from jax import lax
+from jax.experimental import pallas as pl
+from jax.experimental.pallas import tpu as pltpu
 from jax.sharding import PartitionSpec as P
 
 HEADS = 12
 HEAD_DIM = 64
-MB_CAPS = 1
-MICRO = 4
+MB_CAPS = 4
+MICRO = 1
 
 
 EPS = 1e-05
@@ -210,6 +212,676 @@
     dhidden, gain_grad, shift_grad = norm_back(dentry, normed, inverse, cross[0])
     parts = (gain_grad, shift_grad, query_grad, column_sum(dquery), out_grad, out_bias_grad)
     return (grad + dhidden, parts, jnp.concatenate([dkeys, dvalues], -1))
+
+
+BF = jnp.bfloat16
+F32 = jnp.float32
+WIDE = 768
+TOKENS = 256
+CAPS = 4
+SLOT = 64
+PAIRS = 6
+MESH = pl.DeviceIdType.MESH
+RING = 5
+LEAD = (2, 2, 2, 2)
+
+
+def nn(a, b):
+    return lax.dot_general(a, b, (((1,), (0,)), ((), ())), preferred_element_type=F32)
+
+
+def nt(a, b):
+    return lax.dot_general(a, b, (((1,), (1,)), ((), ())), preferred_element_type=F32)
+
+
+def tn(a, b):
+    return lax.dot_general(a, b, (((0,), (0,)), ((), ())), preferred_element_type=F32)
+
+
+def rows_of(i, size):
+    return pl.ds(pl.multiple_of(i * size, size), size)
+
+
+def erf(x):
+    return lax.erf(x)
+
+
+def norm_rows(source, gain, shift, normed, inverse, entry):
+    @pl.loop(0, TOKENS // 32)
+    def _(i):
+        r = rows_of(i, 32)
+        x = source[r, :]
+        centred = x - jnp.mean(x, -1, keepdims=True)
+        inv = lax.rsqrt(jnp.mean(centred * centred, -1, keepdims=True) + EPS)
+        n = centred * inv
+        normed[r, :] = n.astype(normed.dtype)
+        inverse[r, :] = inv
+        entry[r, :] = (n * gain[...] + shift[...]).astype(BF)
+
+
+def norm_rows_back(grad_entry, normed, inverse, gain, grad, vec, gain_row, shift_row):
+    zero = jnp.zeros((8, WIDE), F32)
+
+    def block(i, sums):
+        r = rows_of(i, 32)
+        d = grad_entry[r, :]
+        n = normed[r, :].astype(F32)
+        scaled = d * gain[...]
+        first = jnp.mean(scaled, -1, keepdims=True)
+        second = jnp.mean(scaled * n, -1, keepdims=True)
+        grad[r, :] = grad[r, :] + inverse[r, :] * (scaled - first - n * second)
+        dn = d * n
+        return (
+            sums[0] + jnp.sum(dn.reshape(4, 8, WIDE), 0),
+            sums[1] + jnp.sum(d.reshape(4, 8, WIDE), 0),
+        )
+
+    by_gain, by_shift = lax.fori_loop(0, TOKENS // 32, block, (zero, zero))
+    vec[gain_row : gain_row + 1, :] = jnp.sum(by_gain, 0, keepdims=True)
+    vec[shift_row : shift_row + 1, :] = jnp.sum(by_shift, 0, keepdims=True)
+
+
+def sum_columns(rows, count):
+    def block(i, total):
+        for k in range(count):
+            part = rows(k, rows_of(i, 32)).astype(F32)
+            total = total + jnp.sum(part.reshape(4, 8, WIDE), 0)
+        return total
+
+    total = lax.fori_loop(0, TOKENS // 32, block, jnp.zeros((8, WIDE), F32))
+    return jnp.sum(total, 0, keepdims=True)
+
+
+def mega_kernel(
+    lengths, tokens, cotangent, images,
+    again, ashift, qbias, vbias, obias, fgain, fshift, ebias, rbias,
+    cgain, cshift, cqbias, cvbias, cobias,
+    h_proj, h_out, h_exp, h_red, h_cq, h_ck, h_cv, h_co,
+    out_h, out_in, out_img, out_shards, out_vec,
+    GG, WP, WO, WC, R0, R1, R2, R3,
+    H, G, D, N1, N2, N3, I1, I2, I3, E, ET1, ET2, ET3,
+    QKV, M, MT, QC, C, CT, U, SL, A, AT, PT, PC, IM, IMT, KV, B1, B2, B3, DM,
+    HB, HIN, DIN, DIM, MASK, VL, YS,
+    wsem, lsem, osem, ysend, yrecv, send_sem, recv_sem, vsend, vrecv, credit,
+):
+    section = lax.axis_index("section")
+    dp = lax.axis_index("dp")
+    one = section == 0
+    two = section == 1
+    bits = [lax.rem(lax.div(dp, 1 << k), 2) for k in range(4)]
+    partners = [dp + (1 << k) * (1 - 2 * bits[k]) for k in range(4)]
+    count = jnp.where(two, 16, 12)
+
+    barrier = pltpu.get_barrier_semaphore()
+    for partner in partners:
+        pl.semaphore_signal(barrier, inc=1, device_id={"dp": partner}, device_id_type=MESH)
+    pl.semaphore_signal(barrier, inc=1, device_id={"section": 1 - section}, device_id_type=MESH)
+    pl.semaphore_wait(barrier, 5)
+
+    def across(source, target, i):
+        return pltpu.make_async_remote_copy(
+            src_ref=source, dst_ref=target, send_sem=ysend.at[i], recv_sem=yrecv.at[i],
+            device_id={"section": 1 - section}, device_id_type=MESH,
+        )
+
+    images_a = across(images.at[0:2], IM.at[0:2, 0], 0)
+    images_b = across(images.at[2:4], IM.at[2:4, 0], 1)
+    send_h = across(HB, HIN, 2)
+    send_d = across(HB, DIN, 3)
+    send_i = across(IM.at[:, 0], DIM, 4)
+
+    def load(source, target, i):
+        return pltpu.make_async_copy(source, target, wsem.at[i])
+
+    own_images = load(images, IM.at[:, 1], 0)
+    loads = {
+        "cross": [load(w, WC.at[i], 1 + i) for i, w in enumerate((h_cq, h_ck, h_cv, h_co))],
+        "proj": [load(h_proj, WP, 5)],
+        "out": [load(h_out, WO, 6)],
+        "exp": [
+            load(h_exp.at[:, :, :, :, :, pl.ds(WIDE * j, WIDE)], GG.at[12 + j], 7 + j)
+            for j in range(4)
+        ],
+        "red": [load(h_red.at[j], GG.at[8 + j], 11 + j) for j in range(4)],
+    }
+
+    @pl.when(one)
+    def _():
+        images_a.start()
+
+    @pl.when(two)
+    def _():
+        own_images.start()
+        for i in (1, 2, 0, 3):
+            loads["cross"][i].start()
+
+    for name in ("proj", "out", "exp", "red"):
+        for copy in loads[name]:
+            copy.start()
+
+    def arrived(name):
+        for copy in loads[name]:
+            copy.wait()
+
+    out_vec[...] = jnp.zeros_like(out_vec)
+    low_lane = lax.broadcasted_iota(jnp.int32, (1, 128), 1) < SLOT
+    keep_low = low_lane.astype(F32).astype(BF)
+    keep_high = jnp.logical_not(low_lane).astype(F32).astype(BF)
+
+    def stacked(x):
+        return jnp.concatenate([x * keep_low, x * keep_high], 0)
+
+    def unstacked(x):
+        half = x.shape[0] // 2
+        return jnp.where(low_lane, x[:half], x[half:])
+
+    eighth = jnp.asarray(0.125, BF)
+
+    for pair in range(2):
+        key = lax.broadcasted_iota(jnp.int32, (128, 256), 0)
+        query = lax.rem(lax.broadcasted_iota(jnp.int32, (128, 256), 1), 128)
+        first = key < SLOT
+        length = jnp.where(first, lengths[2 * pair], lengths[2 * pair + 1] + SLOT)
+        same = first == (query < SLOT)
+        MASK[pair] = jnp.where(same & (key <= query) & (key < length), 1.0, 0.0)
+
+    def pair_rows(which, half):
+        rows = IM[2 * which : 2 * which + 2, half].reshape(TOKENS, WIDE)
+        keys = nn(rows, WC[1])
+        KV[2 * which : 2 * which + 2, half, :, :WIDE] = keys.astype(BF).reshape(2, 128, WIDE)
+        values = nn(rows, WC[2]) + cvbias[...]
+        KV[2 * which : 2 * which + 2, half, :, WIDE:] = values.astype(BF).reshape(2, 128, WIDE)
+
+    def turn_images(which, half):
+        for c in (2 * which, 2 * which + 1):
+            IMT[:, pl.ds(c * 256 + 128 * half, 128)] = IM[c, half].T
+
+    @pl.when(two)
+    def _():
+        for copy in loads["cross"]:
+            copy.wait()
+        own_images.wait()
+        for which in range(2):
+            pair_rows(which, 1)
+            turn_images(which, 1)
+        images_a.wait_recv()
+        pair_rows(0, 0)
+        turn_images(0, 0)
+        send_h.wait_recv()
+        H[...] = HIN[...].astype(F32)
+
+    @pl.when(one)
+    def _():
+        H[...] = tokens[...].astype(F32)
+
+    norm_rows(H, again, ashift, N1, I1, E)
+    ET1[...] = E[...].T
+    arrived("proj")
+    QKV[0] = (nn(E[...], WP[:, 0:WIDE]) + qbias[...]).astype(BF)
+    QKV[1] = nn(E[...], WP[:, WIDE : 2 * WIDE]).astype(BF)
+    QKV[2] = (nn(E[...], WP[:, 2 * WIDE :]) + vbias[...]).astype(BF)
+
+    def softmax_keys(scores):
+        expo = jnp.exp(scores - jnp.max(scores, 0, keepdims=True))
+        return expo * (1.0 / jnp.sum(expo, 0, keepdims=True))
+
+    @pl.loop(0, PAIRS)
+    def _(hp):
+        cols = rows_of(hp, 128)
+        for pair in range(2):
+            rows = pl.ds(pair * 128, 128)
+            query = stacked(QKV[0, rows, cols] * eighth)
+            scores = nt(QKV[1, rows, cols], query)
+            scores = jnp.where(MASK[pair] > 0.0, scores, NEG)
+            probs = softmax_keys(scores).astype(BF)
+            PT[2 * hp + pair] = probs
+            M[rows, cols] = unstacked(tn(probs, QKV[2, rows, cols])).astype(BF)
+
+    MT[...] = M[...].T
+    arrived("out")
+    H[...] = H[...] + (nn(M[...], WO[...]) + obias[...])
+
+    @pl.when(two)
+    def _():
+        norm_rows(H, cgain, cshift, N2, I2, E)
+        ET2[...] = E[...].T
+        QC[...] = (nn(E[...], WC[0]) + cqbias[...]).astype(BF)
+        images_b.wait_recv()
+        pair_rows(1, 0)
+        turn_images(1, 0)
+
+        @pl.loop(0, PAIRS)
+        def _(hp):
+            cols = rows_of(hp, 128)
+            vcols = pl.ds(pl.multiple_of(WIDE + hp * 128, 128), 128)
+            for c in range(CAPS):
+                rows = pl.ds(c * SLOT, SLOT)
+                query = stacked(QC[rows, cols] * eighth)
+                keys = KV[c, :, :, cols].reshape(256, 128)
+                probs = softmax_keys(nt(keys, query)).astype(BF)
+                PC[4 * hp + c] = probs
+                values = KV[c, :, :, vcols].reshape(256, 128)
+                C[rows, cols] = unstacked(tn(probs, values)).astype(BF)
+
+        CT[...] = C[...].T
+        H[...] = H[...] + (nn(C[...], WC[3]) + cobias[...])
+
+    norm_rows(H, fgain, fshift, N3, I3, E)
+    ET3[...] = E[...].T
+    arrived("exp")
+    arrived("red")
+    H[...] = H[...] + rbias[...]
+
+    @pl.loop(0, 4)
+    def _(j):
+        U[...] = nn(E[...], GG[12 + j].reshape(WIDE, WIDE)) + ebias[:, rows_of(j, WIDE)]
+
+        @pl.loop(0, TOKENS // 16)
+        def _(i):
+            r = rows_of(i, 16)
+            u = U[r, :]
+            cdf = 0.5 * (1.0 + erf(u * 0.7071067811865476))
+            A[r, :] = (u * cdf).astype(BF)
+            SL[j, r, :] = (cdf + u * jnp.exp(-0.5 * u * u) * 0.3989422804014327).astype(BF)
+
+        AT[rows_of(j, 4)] = A[...].T.reshape(4, 4, 48, TOKENS)
+        H[...] = H[...] + nn(A[...], GG[8 + j].reshape(WIDE, WIDE))
+
+    HB[...] = H[...].astype(BF)
+    store_h = pltpu.make_async_copy(HB, out_h, osem.at[0])
+    store_h.start()
+
+    @pl.when(one)
+    def _():
+        send_h.start()
+        send_h.wait_send()
+        images_a.wait_send()
+        images_b.start()
+
+    @pl.loop(0, CAPS)
+    def _(c):
+        r = rows_of(c, SLOT)
+        live = lax.broadcasted_iota(jnp.int32, (SLOT, 1), 0) < lengths[c]
+        G[r, :] = jnp.where(live, cotangent[r, :].astype(F32), 0.0)
+
+    @pl.when(one)
+    def _():
+        send_d.wait_recv()
+        G[...] = G[...] + DIN[...].astype(F32)
+
+    def where(c, k, bit):
+        return (c,) + tuple(bits[a] if a < k else bit if a == k else slice(None) for a in (3, 2, 1, 0))
+
+    landing = (R0, R1, R2, R3)
+    rings = (RING, RING, 16, 16)
+
+    def exchange(c, k):
+        return pltpu.make_async_remote_copy(
+            src_ref=GG.at[where(c, k, 1 - bits[k])],
+            dst_ref=landing[k].at[lax.rem(c, rings[k])],
+            send_sem=send_sem.at[c, k], recv_sem=recv_sem.at[c, k],
+            device_id={"dp": partners[k]}, device_id_type=MESH,
+        )
+
+    def begin(c, k):
+        if rings[k] < 16:
+            @pl.when(c >= rings[k])
+            def _():
+                pl.semaphore_wait(credit.at[k], 1)
+        exchange(c, k).start()
+
+    def finish(c, k):
+        exchange(c, k).wait()
+        keep = GG.at[where(c, k, bits[k])]
+        term = landing[k].at[lax.rem(c, rings[k])]
+        if k == 3:
+            keep[...] = keep[...] + term[...]
+        elif k == 2:
+            for i in range(2):
+                keep[i] = keep[i] + term[i]
+        elif k == 1:
+            @pl.loop(0, 2)
+            def _(i):
+                for j in range(2):
+                    keep[i, j] = keep[i, j] + term[i, j]
+        else:
+            @pl.loop(0, 4)
+            def _(i):
+                for j in range(2):
+                    a, b = lax.div(i, 2), lax.rem(i, 2)
+                    keep[a, b, j] = keep[a, b, j] + term[a, b, j]
+        if rings[k] < 16:
+            @pl.when(c + rings[k] < count)
+            def _():
+                pl.semaphore_signal(
+                    credit.at[k], inc=1, device_id={"dp": partners[k]}, device_id_type=MESH
+                )
+
+    def weight_gradient(c, left, right):
+        for t in range(3):
+            part = nn(left, right(pl.ds(256 * t, 256)))
+            GG[c, :, :, :, :, :, pl.ds(256 * t, 256)] = part.astype(BF).reshape(LEAD + (48, 256))
+
+    B1[...] = G[...].astype(BF)
+    out_vec[7:8, :] = sum_columns(lambda k, r: B1[r, :], 1)
+
+    @pl.loop(0, 4)
+    def _(i):
+        weight_gradient(i, AT[:, i].reshape(WIDE, TOKENS), lambda t: B1[:, t])
+        begin(i, 0)
+
+    @pl.loop(0, 4)
+    def _(j):
+        U[...] = nt(B1[...], GG[8 + j].reshape(WIDE, WIDE))
+
+        def block(i, total):
+            r = rows_of(i, 32)
+            du = (U[r, :] * SL[j, r, :].astype(F32)).astype(BF)
+            SL[j, r, :] = du
+            return total + jnp.sum(du.astype(F32).reshape(4, 8, WIDE), 0)
+
+        total = lax.fori_loop(0, TOKENS // 32, block, jnp.zeros((8, WIDE), F32))
+        out_vec[pl.ds(8 + j, 1), :] = jnp.sum(total, 0, keepdims=True)
+        part = nt(SL[j], GG[12 + j].reshape(WIDE, WIDE))
+
+        @pl.when(j == 0)
+        def _():
+            D[...] = part
+
+        @pl.when(j > 0)
+        def _():
+            D[...] = D[...] + part
+
+    norm_rows_back(D, N3, I3, fgain, G, out_vec, 5, 6)
+
+    @pl.loop(0, 4)
+    def _(i):
+        finish(i, 0)
+        begin(i, 1)
+
+    @pl.when(two)
+    def _():
+        B2[...] = G[...].astype(BF)
+        out_vec[16:17, :] = sum_columns(lambda k, r: B2[r, :], 1)
+        DM[...] = nt(B2[...], WC[3]).astype(BF)
+
+        @pl.loop(0, PAIRS)
+        def _(hp):
+            cols = rows_of(hp, 128)
+            vcols = pl.ds(pl.multiple_of(WIDE + hp * 128, 128), 128)
+            for c in range(CAPS):
+                rows = pl.ds(c * SLOT, SLOT)
+                query = stacked(QC[rows, cols] * eighth)
+                grad = stacked(DM[rows, cols])
+                keys = KV[c, :, :, cols].reshape(256, 128)
+                values = KV[c, :, :, vcols].reshape(256, 128)
+                probs = PC[4 * hp + c]
+                wide = probs.astype(F32)
+                dprobs = nt(values, grad)
+                dscores = (wide * (dprobs - jnp.sum(wide * dprobs, 0, keepdims=True))).astype(BF)
+                KV[c, :, :, cols] = nn(dscores, query).astype(BF).reshape(2, 128, 128)
+                KV[c, :, :, vcols] = nn(probs, grad).astype(BF).reshape(2, 128, 128)
+                QC[rows, cols] = (unstacked(tn(dscores, keys)) * 0.125).astype(BF)
+
+        out_vec[14:15, :] = sum_columns(lambda k, r: QC[r, :], 1)
+        D[...] = nt(QC[...], WC[0])
+        norm_rows_back(D, N2, I2, cgain, G, out_vec, 12, 13)
+
+    B3[...] = G[...].astype(BF)
+    out_vec[4:5, :] = sum_columns(lambda k, r: B3[r, :], 1)
+    DM[...] = nt(B3[...], WO[...]).astype(BF)
+
+    @pl.loop(0, PAIRS)
+    def _(hp):
+        cols = rows_of(hp, 128)
+        for pair in range(2):
+            rows = pl.ds(pair * 128, 128)
+            query = stacked(QKV[0, rows, cols] * eighth)
+            grad = stacked(DM[rows, cols])
+            keys = QKV[1, rows, cols]
+            probs = PT[2 * hp + pair]
+            wide = probs.astype(F32)
+            dprobs = nt(QKV[2, rows, cols], grad)
+            dscores = (wide * (dprobs - jnp.sum(wide * dprobs, 0, keepdims=True))).astype(BF)
+            QKV[1, rows, cols] = nn(dscores, query).astype(BF)
+            QKV[2, rows, cols] = nn(probs, grad).astype(BF)
+            QKV[0, rows, cols] = (unstacked(tn(dscores, keys)) * 0.125).astype(BF)
+
+    out_vec[2:3, :] = sum_columns(lambda k, r: QKV[0, r, :], 1)
+    out_vec[3:4, :] = sum_columns(lambda k, r: QKV[2, r, :], 1)
+    D[...] = nt(QKV[0], WP[:, 0:WIDE])
+    D[...] = D[...] + nt(QKV[1], WP[:, WIDE : 2 * WIDE])
+    D[...] = D[...] + nt(QKV[2], WP[:, 2 * WIDE :])
+    norm_rows_back(D, N1, I1, again, G, out_vec, 0, 1)
+
+    store_h.wait()
+
+    @pl.when(two)
+    def _():
+        HB[...] = G[...].astype(BF)
+        send_d.start()
+        G[...] = HB[...].astype(F32)
+
+    store_in = pltpu.make_async_copy(G, out_in, osem.at[1])
+    store_in.start()
+
+    @pl.loop(0, 4)
+    def _(j):
+        weight_gradient(4 + j, ET3[...], lambda t: SL[j, :, t])
+        begin(4 + j, 0)
+
+    @pl.loop(0, 3)
+    def _(j):
+        weight_gradient(8 + j, ET1[...], lambda t: QKV[j, :, t])
+
+    weight_gradient(11, MT[...], lambda t: B3[:, t])
+
+    @pl.when(two)
+    def _():
+        weight_gradient(12, ET2[...], lambda t: QC[:, t])
+        for j in range(2):
+            weight_gradient(
+                13 + j, IMT[...],
+                lambda t: KV[:, :, :, pl.ds(WIDE * j + t.start, t.size)].reshape(4 * 256, t.size),
+            )
+        weight_gradient(15, CT[...], lambda t: B2[:, t])
+        out_vec[15:16, :] = sum_columns(
+            lambda k, r: KV[k, :, pl.ds(pl.multiple_of(lax.div(r.start, 2), 16), 16), WIDE:].reshape(32, WIDE), 4
+        )
+        for c in range(CAPS):
+            part = nt(KV[c, :, :, :WIDE].reshape(256, WIDE), WC[1])
+            part = part + nt(KV[c, :, :, WIDE:].reshape(256, WIDE), WC[2])
+            IM[c] = part.astype(BF).reshape(2, 128, WIDE)
+        send_i.start()
+
+    for k in range(4):
+        copy = pltpu.make_async_remote_copy(
+            src_ref=out_vec, dst_ref=VL.at[k], send_sem=vsend.at[k], recv_sem=vrecv.at[k],
+            device_id={"dp": partners[k]}, device_id_type=MESH,
+        )
+        copy.start()
+        copy.wait()
+        out_vec[...] = out_vec[...] + VL[k]
+
+    def shard_out(c):
+        return pltpu.make_async_copy(
+            GG.at[(c,) + tuple(bits[a] for a in (3, 2, 1, 0))], out_shards.at[c], lsem.at[c]
+        )
+
+    def shard_across(c):
+        return across(GG.at[(c,) + tuple(bits[a] for a in (3, 2, 1, 0))], YS.at[c - 12], 6 + c - 12)
+
+    @pl.loop(0, count + 2)
+    def _(tick):
+        ahead = tick + 5
+
+        @pl.when((ahead >= 8) & (ahead < count))
+        def _():
+            begin(ahead, 0)
+
+        @pl.when(tick + 4 < count)
+        def _():
+            finish(tick + 4, 0)
+            begin(tick + 4, 1)
+
+        @pl.when(tick < count)
+        def _():
+            finish(tick, 1)
+            begin(tick, 2)
+
+        @pl.when((tick >= 1) & (tick - 1 < count))
+        def _():
+            finish(tick - 1, 2)
+            begin(tick - 1, 3)
+
+        @pl.when((tick >= 2) & (tick - 2 < count))
+        def _():
+            finish(tick - 2, 3)
+            shard_out(tick - 2).start()
+
+            @pl.when(tick - 2 >= 12)
+            def _():
+                shard_across(tick - 2).start()
+
+    @pl.when(two)
+    def _():
+        vec_copy = across(out_vec, VL.at[4], 5)
+        vec_copy.start()
+        vec_copy.wait_send()
+        store_img = pltpu.make_async_copy(IM.at[:, 1], out_img, osem.at[2])
+        store_img.start()
+        store_img.wait()
+        send_d.wait_send()
+        send_i.wait_send()
+        for c in range(12, 16):
+            shard_across(c).wait_send()
+
+    @pl.when(one)
+    def _():
+        images_b.wait_send()
+        send_i.wait_recv()
+        store_img = pltpu.make_async_copy(DIM, out_img, osem.at[2])
+        store_img.start()
+        across(out_vec, VL.at[4], 5).wait_recv()
+        out_vec[12:17, :] = VL[4, 12:17, :]
+        store_img.wait()
+        for c in range(12, 16):
+            across(YS.at[c - 12], YS.at[c - 12], 6 + c - 12).wait_recv()
+            copy = pltpu.make_async_copy(YS.at[c - 12], out_shards.at[c], lsem.at[c])
+            copy.start()
+            copy.wait()
+
+    store_in.wait()
+
+    @pl.loop(0, count)
+    def _(c):
+        shard_out(c).wait()
+
+
+def mega(args):
+    (
+        tokens, images, lengths, cotangent, again, ashift, proj, qb, vb, wo, ob, fg, fs, we, eb, wr, rb,
+        cg, cs, cq, cqb, ck, cv, cvb, co, cob,
+    ) = args
+    row = lambda v: v.reshape(1, -1)
+    vm = pl.BlockSpec(memory_space=pltpu.VMEM)
+    hbm = pl.BlockSpec(memory_space=pl.ANY)
+    operands = [
+        (lengths, pl.BlockSpec(memory_space=pltpu.SMEM)),
+        (tokens.reshape(TOKENS, WIDE), vm),
+        (cotangent.reshape(TOKENS, WIDE), vm),
+        (images, hbm),
+    ]
+    operands += [(row(v), vm) for v in (again, ashift, qb, vb, ob, fg, fs, eb, rb, cg, cs, cqb, cvb, cob)]
+    operands += [
+        (proj[0], hbm), (wo[0], hbm),
+        (we.reshape(LEAD + (48, 4 * WIDE)), hbm), (wr.reshape((4,) + LEAD + (48, WIDE)), hbm),
+        (cq, hbm), (ck, hbm), (cv, hbm), (co, hbm),
+    ]
+    s = jax.ShapeDtypeStruct
+    dma = pltpu.SemaphoreType.DMA
+    big = (TOKENS, WIDE)
+    turned = (WIDE, TOKENS)
+    b = lambda *shape: pltpu.VMEM(shape, BF)
+    f = lambda *shape: pltpu.VMEM(shape, F32)
+    return pl.pallas_call(
+        mega_kernel,
+        out_shape=(
+            s(big, BF), s(big, F32), s((CAPS, 128, WIDE), BF), s((16, 48, WIDE), BF), s((24, WIDE), F32),
+        ),
+        in_specs=[spec for _, spec in operands],
+        out_specs=[hbm, hbm, hbm, hbm, vm],
+        scratch_shapes=[
+            b(16, *LEAD, 48, WIDE), b(WIDE, 3 * WIDE), b(WIDE, WIDE), b(4, WIDE, WIDE),
+            b(RING, 2, 2, 2, 48, WIDE), b(RING, 2, 2, 48, WIDE), b(16, 2, 48, WIDE), b(16, 48, WIDE),
+            f(*big), f(*big), f(*big), b(*big), b(*big), b(*big), f(TOKENS, 1), f(TOKENS, 1), f(TOKENS, 1),
+            b(*big), b(*turned), b(*turned), b(*turned),
+            b(3, *big), b(*big), b(*turned), b(*big), b(*big), b(*turned), f(*big), b(4, *big), b(*big),
+            b(16, 4, 48, TOKENS), b(12, 128, 256), b(24, 256, 128), b(CAPS, 2, 128, WIDE), b(WIDE, 1024),
+            b(CAPS, 2, 128, 2 * WIDE), b(*big), b(*big), b(*big), b(*big),
+            b(*big), b(*big), b(*big), b(CAPS, 128, WIDE), f(2, 128, 256), f(5, 24, WIDE), b(4, 48, WIDE),
+            dma((15,)), dma((16,)), dma((3,)), dma((10,)), dma((10,)),
+            dma((16, 4)), dma((16, 4)), dma((4,)), dma((4,)), pltpu.SemaphoreType.REGULAR((2,)),
+        ],
+        compiler_params=pltpu.CompilerParams(
+            collective_id=0, has_side_effects=True, vmem_limit_bytes=63 * 2**20
+        ),
+        name="layers",
+    )(*[x for x, _ in operands])
+
+
+def finish_kernel(dp_ref, h, gin, img, shards, vec, *outs):
+    (
+        o_h, o_in, o_img, o_ag, o_as, o_proj, o_qb, o_vb, o_wo, o_ob, o_fg, o_fs, o_we, o_eb, o_wr, o_rb,
+        o_cg, o_cs, o_cq, o_cqb, o_ck, o_cv, o_cvb, o_co, o_cob,
+    ) = outs
+    dp = dp_ref[0]
+    o_h[...] = h[...].reshape(o_h.shape)
+    o_in[...] = gin[...].reshape(o_in.shape)
+    o_img[...] = img[...].astype(F32)
+    for j in range(3):
+        o_proj[0, :, WIDE * j : WIDE * (j + 1)] = shards[8 + j].astype(F32)
+    o_wo[0] = shards[11].astype(F32)
+    for j in range(4):
+        o_we[0, :, WIDE * j : WIDE * (j + 1)] = shards[4 + j].astype(F32)
+        o_wr[0, 48 * j : 48 * (j + 1), :] = shards[j].astype(F32)
+    for j, out in enumerate((o_cq, o_ck, o_cv, o_co)):
+        out[...] = shards[12 + j].astype(F32)
+    mine = pltpu.roll(vec[...], WIDE - 48 * dp, 1)
+    places = (
+        (o_ag, 0), (o_as, 1), (o_qb, 2), (o_vb, 3), (o_ob, 4), (o_fg, 5), (o_fs, 6), (o_rb, 7),
+        (o_cg, 12), (o_cs, 13), (o_cqb, 14), (o_cvb, 15), (o_cob, 16),
+    )
+    for out, i in places:
+        out[...] = mine[i : i + 1, :48]
+    part = lax.rem(dp, 4)
+    own = pltpu.roll(vec[8:16, :], WIDE - 192 * part, 1)[:4, :192]
+    chosen = lax.broadcasted_iota(jnp.int32, (4, 192), 0) == lax.div(dp, 4)
+    o_eb[...] = jnp.sum(jnp.where(chosen, own, 0.0), 0, keepdims=True)
+
+
+def finish_outputs(parts):
+    vm = pl.BlockSpec(memory_space=pltpu.VMEM)
+    small = (1, 48)
+    shapes = [
+        (1, CAPS, SLOT, WIDE), (1, CAPS, SLOT, WIDE), (CAPS, 128, WIDE),
+        small, small, (1, 48, 3 * WIDE), small, small, (1, 48, WIDE), small, small, small,
+        (1, 48, 4 * WIDE), (1, 192), (1, 192, WIDE), small,
+        small, small, (48, WIDE), small, (48, WIDE), (48, WIDE), small, (48, WIDE), small,
+    ]
+    dp = lax.axis_index("dp").astype(jnp.int32).reshape(1)
+    outs = pl.pallas_call(
+        finish_kernel,
+        out_shape=[jax.ShapeDtypeStruct(x, BF if i == 0 else F32) for i, x in enumerate(shapes)],
+        in_specs=[pl.BlockSpec(memory_space=pltpu.SMEM)] + [vm] * 5,
+        out_specs=[vm] * 25,
+        compiler_params=pltpu.CompilerParams(vmem_limit_bytes=40 * 2**20),
+        name="finish",
+    )(dp, *parts)
+    outs = list(outs)
+    for i in (16, 17, 19, 22, 24):
+        outs[i] = outs[i].reshape(-1)
+    return tuple(outs)
 
 
 def body(
@@ -395,6 +1067,10 @@
     return (finished[None], input_grads[None], image_grads) + tuple(shared) + tuple(crossed)
 
 
+def one_kernel(*args):
+    return finish_outputs(mega(args))
+
+
 def solution(mesh):
     placed = (
         P("dp", None, None),
@@ -425,7 +1101,7 @@
         P(),
     )
     return jax.shard_map(
-        body,
+        one_kernel if mesh.shape["dp"] == 16 else body,
         mesh=mesh,
         in_specs=placed,
         out_specs=(

time: 1960 us -> 216 us (0.11); the launches traced: 1940 us -> 216 us
  waiting for transfers between devices: 1010 us -> 0 us
  matrix products: 297 us -> 0 us
  local copies, waits for them, and re-layouts: 262 us -> 11.7 us
  Pallas kernels: 0 us -> 203 us
  other arithmetic: 166 us -> 0 us
  starting transfers between devices: 120 us -> 0 us
  blocking collectives: 65.4 us -> 0 us
    reduce_scatter x8 -> x0, waiting for transfers between devices: 544 us -> none  [the longest x4 387 us: body(): lax.psum_scatter(tuple((total[None] for total in layer_sums)), 'dp', scat...]
    dot_general x90 -> x0, matrix products: 297 us -> none  [the longest x20 126 us: weight_product(): jnp.einsum('bsi,bsj->ij', rows, grad, preferred_element_type=jnp.float32)]
    unnamed x27 -> x0, waiting for transfers between devices: 286 us -> none
    pallas_call x0 -> x2, Pallas kernels: none -> 203 us  [the longest x1 201 us: mega(): pl.pallas_call(mega_kernel, out_shape=(s(big, BF), s(big, F32), s((CAPS,...]
    ppermute x16 -> x0, waiting for transfers between devices: 156 us -> none  [shifted(): return lax.ppermute(block, axis, route)]
    ppermute x16 -> x0, starting transfers between devices: 119 us -> none  [shifted(): return lax.ppermute(block, axis, route)]
    another operation x104 -> x0, local copies, waits for them, and re-layouts: 107 us -> none
    unnamed x1 -> x0, blocking collectives: 57.7 us -> none
  transfers between devices with their start and end apart: 34 -> 0, of which waited for: 20 -> 0; matrix products, arithmetic and copies ran while one was open for 24% -> 0% of each run, Pallas kernels for 0% -> 0%
where the time goes in v2:
time: 216 us
  Pallas kernels  203 us (94%)
  local copies, waits for them, and re-layouts  11.7 us (5%)
    pallas_call x1, Pallas kernels, mega(): pl.pallas_call(mega_kernel, out_shape=(s(big, BF), s(big, F32), s((CAPS,...  201 us
    reshape x5, local copies, waits for them, and re-layouts, mega(): row = lambda v: v.reshape(1, -1)  6.33 us
    unnamed x10, local copies, waits for them, and re-layouts  5.41 us

profile of v2, /device:TPU:0, one launch (start us, length us, event | category | flops | bytes accessed | tf_op | source)
XLA Modules:
  0.0 215.6 jit_solution(14722075310667893737)
XLA Ops:
  0.7 1.3 reshape.98.cgain
  1.9 1.3 reshape.99.cshift
  3.2 1.3 reshape.100.cqbias
  4.5 1.3 reshape.101.cvbias
  5.7 1.3 reshape.102.cobias
  7.0 200.6 %layers.1 = (bf16[256,768]{1,0:T(8,128)(2,1)}, f32[256,768]{1,0:T(8,128)}, bf16[4,128,768]{2,1,0:T(8,128)(2,1)}, bf16[16,48,768]{2,1,0:T(8,128)(2,1)}, f32[24,768]{1,0:T(8,128)}) custom-call(s32[4]{0:T(128)} %lengths.1, bf16[256,768]{1,0:T(8,128)(2,1)} %bitcast.16, bf16[256,768]{1,0:T(8,128)(2,1)} %bitcast.17, bf16[4,128,768]{2,1,0:T(8,128)(2,1)} %images.1, ...), custom_call_target="tpu_custom_call" | custom-call | tf_op jit(solution)/shard_map/layers/pallas_call | solution.py:807
  207.7 0.0 copy-start
  207.7 1.3 copy-done
  208.9 0.0 copy-start.1
  208.9 1.1 copy-done.1
  210.1 0.0 copy-start.2
  210.1 1.1 copy-done.2
  211.2 0.0 copy-start.3
  211.2 1.0 copy-done.3
  212.2 0.0 copy-start.4
  212.2 0.9 copy-done.4
  213.1 2.4 %finish.1 = (bf16[1,4,64,768]{3,2,1,0:T(8,128)(2,1)}, f32[1,4,64,768]{3,2,1,0:T(8,128)}, f32[4,128,768]{2,1,0:T(8,128)}, f32[1,48]{1,0:T(1,128)}, f32[1,48]{1,0:...) custom-call(s32[1]{0:T(128)} %bitcast.dp_ref, ...), custom_call_target="tpu_custom_call" | custom-call | tf_op jit(solution)/shard_map/finish/pallas_call | solution.py:873
Async XLA Ops:
  207.7 1.3 copy-start
  208.9 1.1 copy-start.1
  210.1 1.1 copy-start.2
  211.2 1.0 copy-start.3
  212.2 0.9 copy-start.4
